TPU v7x, 128 devices: a whole 4x4x4 slice. The times are simulated.
128 devices in a mesh: pp: 2 (over y_hi), ep: 64 (over x, y_lo, z, core).
Axes of the slice: x: 4, y: 4 (y_hi: 2, y_lo: 2; y = y_hi * 2 + y_lo), z: 4, core: 2. Of those that a mesh axis runs over, the one named last changes fastest.
Arguments:
- entering: bfloat16 [2, 4096, 7168], P('pp', 'ep'), may hold values from -6 to 6
- norm_gain: float32 [2, 7168], P('pp'), may hold values from 0.1 to 1.9
- routes: int32 [2, 2, 4096, 2], P('pp', None, 'ep'), may hold values from 0 to 31, all different within a row; in each aligned block of 64 rows (0 to 63, 64 to 127, ..., all dimensions but the last counted through in order) at most 6 rows name the same one
- route_gates: float32 [2, 2, 4096, 2], P('pp', None, 'ep'), may hold values from 0.1 to 1
- w_gate: bfloat16 [2, 7168, 32768], P('pp', None, 'ep'), may hold values from -0.0625 to 0.0625
- w_up: bfloat16 [2, 7168, 32768], P('pp', None, 'ep'), may hold values from -0.0625 to 0.0625
- w_down: bfloat16 [2, 32768, 7168], P('pp', 'ep'), may hold values from -0.1875 to 0.1875
Outputs:
- finished: bfloat16 [2, 4096, 7168], P('pp', 'ep')
Inputs may be any that keep to these rules, and one draw needn't show every extreme that they name: `routes`: each row names 2 different experts. In each aligned block of 64 rows of one layer and micro-batch (the rows of one device) no expert is named by more than 6 rows, a bound that some block reaches.
All inputs are finite; a program needn't handle non-finite values.
Results may differ from a plain program's by a relative error of at most 0.0075.
Values may be sent and summed in bfloat16 or wider, within the bound.
No kernel may reach another device: no remote copies, remote signals or barrier semaphores. Data moves between devices by JAX's collectives and lax.ppermute only.
A program may use at most 128 MiB of HBM per device.

v0:
```python
import jax
import jax.numpy as jnp
from jax import lax
from jax.sharding import PartitionSpec as P

SHARDS = 2


epsilon = 1e-06


def partner(value, axis, bit):
    mask = 2**bit
    pairs = [(source, source ^ mask) for source in range(lax.axis_size(axis))]
    return lax.ppermute(value, axis, pairs)


def normalize(token_rows, gain_row):
    widened = token_rows.astype(jnp.float32)
    inv_rms = lax.rsqrt(jnp.mean(widened * widened, axis=1, keepdims=True) + epsilon)
    return (widened * inv_rms * gain_row).astype(jnp.bfloat16)


def place_pairs(chosen, experts, capacity):
    flattened = chosen.reshape(-1)
    onehot = (flattened[:, None] == jnp.arange(experts, dtype=jnp.int32)[None, :]).astype(jnp.int32)
    before = jnp.cumsum(onehot, axis=0) - onehot
    slot_index = jnp.sum(before * onehot, axis=1)
    return flattened * capacity + slot_index


def return_partials(partial_value):
    return lax.all_to_all(partial_value, "ep", split_axis=0, concat_axis=0, tiled=True)


def expert_block(token_rows, gain_row, chosen, pair_gates, w_gate, w_up, w_down):
    token_count, width = token_rows.shape
    topk = chosen.shape[1]
    devices = lax.axis_size("ep")
    experts = devices // SHARDS
    capacity = 3 * token_count * topk // (2 * experts)
    normed = normalize(token_rows, gain_row)
    position = place_pairs(chosen, experts, capacity)
    source_row = (
        jnp.full((experts * capacity,), token_count, jnp.int32)
        .at[position]
        .set(jnp.arange(token_count * topk, dtype=jnp.int32) // topk)
    )
    padded = jnp.concatenate([normed, jnp.zeros((1, width), jnp.bfloat16)], axis=0)

    def expert_rows(received):
        stacked = received.reshape(-1, width)
        gate_act = jnp.dot(stacked, w_gate, preferred_element_type=jnp.float32)
        up_act = jnp.dot(stacked, w_up, preferred_element_type=jnp.float32)
        hidden = (jax.nn.silu(gate_act) * up_act).astype(jnp.bfloat16)
        partial_value = jnp.dot(hidden, w_down, preferred_element_type=jnp.float32).astype(
            jnp.bfloat16
        )
        return partial_value.reshape(received.shape)

    sources = jnp.repeat(source_row.reshape(experts, capacity), SHARDS, axis=0)
    outgoing = padded[sources]
    returned = (lambda arrived_rows: return_partials(expert_rows(arrived_rows)))(
        lax.all_to_all(outgoing, "ep", split_axis=0, concat_axis=0, tiled=True)
    )
    summed = returned.reshape(experts, SHARDS, capacity, width).astype(jnp.float32).sum(axis=1)
    summed = lax.optimization_barrier(summed.astype(jnp.bfloat16))
    summed = summed.reshape(experts * capacity, width)
    picked = summed[position].astype(jnp.float32).reshape(token_count, topk, width)
    combined = token_rows.astype(jnp.float32) + jnp.sum(pair_gates[:, :, None] * picked, axis=1)
    return combined.astype(jnp.bfloat16)


def shards(entering, norm_gain, routes, route_gates, w_gate, w_up, w_down):
    section = lax.axis_index("pp")

    def run_segment(token_rows, micro_batch):
        chosen = lax.dynamic_index_in_dim(routes[0], micro_batch, 0, keepdims=False)
        pair_gates = lax.dynamic_index_in_dim(route_gates[0], micro_batch, 0, keepdims=False)
        return expert_block(
            token_rows, norm_gain[0], chosen, pair_gates, w_gate[0], w_up[0], w_down[0]
        )

    moved = run_segment(entering[0], section)
    arrived = partner(moved, "pp", 0)
    finished = run_segment(arrived, 1 - section)
    return finished[None]


def solution(mesh):
    return jax.shard_map(
        shards,
        mesh=mesh,
        in_specs=(
            P("pp", "ep", None),
            P("pp", None),
            P("pp", None, "ep", None),
            P("pp", None, "ep", None),
            P("pp", None, "ep"),
            P("pp", None, "ep"),
            P("pp", "ep", None),
        ),
        out_specs=P("pp", "ep", None),
        check_vma=False,
    )
```

profile of v0, /device:TPU:0, one launch (start us, length us, event | category | flops | bytes accessed | tf_op | source)
XLA Modules:
  0.0 584.3 jit_solution(2734375707011326967)
XLA Ops:
  3.8 1.5 fusion.14
  5.3 1.5 fusion.16
  6.9 6.5 %gather_fusion = bf16[384,7168]{1,0:T(8,128)(2,1)} fusion(bf16[65,7168]{1,0:T(8,128)(2,1)S(1)} %concatenate.6, s32[1024]{0:T(1024)S(1)} %pad_clamp_fusion.3), kind=kCustom, calls=%fused_computation | custom fusion | bytes 11011584 | tf_op jit(solution)/shard_map/gather | solution.py:62
  13.3 8.3 %reshape.210 = bf16[64,6,7168]{2,1,0:T(8,128)(2,1)} reshape(bf16[384,7168]{1,0:T(8,128)(2,1)} %gather_fusion) | data formatting | bytes 11010048 | tf_op jit(solution)/shard_map/gather | solution.py:62
  21.7 95.2 %all_to_all.20 = bf16[64,6,7168]{2,1,0:T(8,128)(2,1)} all-to-all(bf16[64,6,7168]{2,1,0:T(8,128)(2,1)} %reshape.210), channel_id=1, replica_groups=mesh['pp'=2,'ep'=64] {'ep'}, dimensions={0} | all-to-all | bytes 11010048 | tf_op jit(solution)/shard_map/all_to_all | solution.py:64
  116.9 8.5 %reshape.196 = bf16[384,7168]{1,0:T(8,128)(2,1)} reshape(bf16[64,6,7168]{2,1,0:T(8,128)(2,1)} %all_to_all.20) | data formatting | bytes 11010048 | tf_op jit(solution)/shard_map/reshape | solution.py:52
  125.4 6.9 %fusion.8 = f32[384,512]{1,0:T(8,128)S(1)} fusion(bf16[384,7168]{1,0:T(8,128)(2,1)} %reshape.196, bf16[1,7168,512]{2,1,0:T(8,128)(2,1)} %param.11), kind=kOutput, calls=%fused_computation.18 | convolution fusion | flops 2818572288 | bytes 13631488 | tf_op jit(solution)/shard_map/dot_general | solution.py:53
  132.4 15.1 %convolution_convert_fusion.1 = bf16[384,7168]{1,0:T(8,128)(2,1)} fusion(bf16[1,512,7168]{2,1,0:T(8,128)(2,1)} %param.13, bf16[384,7168]{1,0:T(8,128)(2,1)} %reshape.196, bf16[1,7168,512]{2,1,0:T(8,128)(2,1)} %param.12, f32[384,512]{1,0:T(8,128)S(1)} %fusion.8), kind=kOutput, calls=%fused_computation.7 | convolution fusion | flops 5641076736 | bytes 26476544 | tf_op jit(solution)/shard_map/dot_general | solution.py:56
  147.5 8.3 %reshape.197 = bf16[64,6,7168]{2,1,0:T(8,128)(2,1)} reshape(bf16[384,7168]{1,0:T(8,128)(2,1)} %convolution_convert_fusion.1) | data formatting | bytes 11010048 | tf_op jit(solution)/shard_map/reshape | solution.py:59
  155.8 7.5 %all-to-all-start.1 = ((bf16[64,6,7168]{2,1,0:T(8,128)(2,1)}), bf16[64,6,7168]{2,1,0:T(8,128)(2,1)}, u32[]{:S(2)}, u32[]{:S(2)}) async-start(bf16[64,6,7168]{2,1,0:T(8,128)(2,1)} %reshape.197), calls=%async_computation.1 | async-start | bytes 14680064 | tf_op jit(solution)/shard_map/all_to_all | solution.py:33
  163.4 94.1 %all-to-all-done.1 = bf16[64,6,7168]{2,1,0:T(8,128)(2,1)} async-done(((bf16[64,6,7168]{2,1,0:T(8,128)(2,1)}), bf16[64,6,7168]{2,1,0:T(8,128)(2,1)}, u32[]{:S(2)}, u32[]{:S(2)}) %all-to-all-start.1) | async-done | bytes 5505056 | tf_op jit(solution)/shard_map/all_to_all | solution.py:33
  257.5 7.8 %bitcast_reduce_fusion.1 = bf16[32,6,7168]{2,1,0:T(8,128)(2,1)} fusion(bf16[64,6,7168]{2,1,0:T(8,128)(2,1)} %all-to-all-done.1), kind=kLoop, calls=%fused_computation.9 | loop fusion | flops 1376256 | bytes 8257536 | tf_op jit(solution)/shard_map/reduce_sum | solution.py:66
  265.3 3.2 reshape.199
  268.5 3.0 gather_fusion.1
  271.5 5.3 reshape.207
  276.8 7.1 %multiply_reduce_fusion.1 = f32[64,7168]{1,0:T(8,128)S(1)} fusion(f32[64,2,7168]{2,1,0:T(2,128)} %reshape.207, f32[64,2]{1,0:T(8,128)S(1)} %copy.14), kind=kLoop, calls=%fused_computation.21 | loop fusion | flops 1376256 | bytes 5505536 | tf_op jit(solution)/shard_map/reduce_sum | solution.py:70
  284.2 3.0 collective-permute-start
  288.6 14.7 %collective-permute-done = bf16[64,7168]{1,0:T(8,128)(2,1)S(1)} collective-permute-done((bf16[64,7168]{1,0:T(8,128)(2,1)S(1)}, bf16[64,7168]{1,0:T(8,128)(2,1)S(1)}, u32[]{:S(2)}, u32[]{:S(2)}) %collective-permute-start) | collective-permute-done | bytes 917536 | tf_op jit(solution)/shard_map/ppermute | solution.py:15
  304.6 6.5 %gather_fusion.2 = bf16[384,7168]{1,0:T(8,128)(2,1)} fusion(bf16[65,7168]{1,0:T(8,128)(2,1)S(1)} %concatenate.7, s32[1024]{0:T(1024)S(1)} %pad_clamp_fusion.1), kind=kCustom, calls=%fused_computation.2 | custom fusion | bytes 11011584 | tf_op jit(solution)/shard_map/gather | solution.py:62
  311.0 8.3 %reshape.226 = bf16[64,6,7168]{2,1,0:T(8,128)(2,1)} reshape(bf16[384,7168]{1,0:T(8,128)(2,1)} %gather_fusion.2) | data formatting | bytes 11010048 | tf_op jit(solution)/shard_map/gather | solution.py:62
  319.4 96.6 %all_to_all.21 = bf16[64,6,7168]{2,1,0:T(8,128)(2,1)} all-to-all(bf16[64,6,7168]{2,1,0:T(8,128)(2,1)} %reshape.226), channel_id=1, replica_groups=mesh['pp'=2,'ep'=64] {'ep'}, dimensions={0} | all-to-all | bytes 11010048 | tf_op jit(solution)/shard_map/all_to_all | solution.py:64
  416.0 8.5 %reshape.202 = bf16[384,7168]{1,0:T(8,128)(2,1)} reshape(bf16[64,6,7168]{2,1,0:T(8,128)(2,1)} %all_to_all.21) | data formatting | bytes 11010048 | tf_op jit(solution)/shard_map/reshape | solution.py:52
  424.5 6.9 %fusion.6 = f32[384,512]{1,0:T(8,128)S(1)} fusion(bf16[384,7168]{1,0:T(8,128)(2,1)} %reshape.202, bf16[1,7168,512]{2,1,0:T(8,128)(2,1)} %param.11), kind=kOutput, calls=%fused_computation.16 | convolution fusion | flops 2818572288 | bytes 13631488 | tf_op jit(solution)/shard_map/dot_general | solution.py:53
  431.5 15.1 %convolution_convert_fusion = bf16[384,7168]{1,0:T(8,128)(2,1)} fusion(bf16[1,512,7168]{2,1,0:T(8,128)(2,1)} %param.13, bf16[384,7168]{1,0:T(8,128)(2,1)} %reshape.202, bf16[1,7168,512]{2,1,0:T(8,128)(2,1)} %param.12, f32[384,512]{1,0:T(8,128)S(1)} %fusion.6), kind=kOutput, calls=%fused_computation.6 | convolution fusion | flops 5641076736 | bytes 26476544 | tf_op jit(solution)/shard_map/dot_general | solution.py:56
  446.6 8.3 %reshape.203 = bf16[64,6,7168]{2,1,0:T(8,128)(2,1)} reshape(bf16[384,7168]{1,0:T(8,128)(2,1)} %convolution_convert_fusion) | data formatting | bytes 11010048 | tf_op jit(solution)/shard_map/reshape | solution.py:59
  454.9 7.5 %all-to-all-start.3 = ((bf16[64,6,7168]{2,1,0:T(8,128)(2,1)}), bf16[64,6,7168]{2,1,0:T(8,128)(2,1)}, u32[]{:S(2)}, u32[]{:S(2)}) async-start(bf16[64,6,7168]{2,1,0:T(8,128)(2,1)} %reshape.203), calls=%async_computation.3 | async-start | bytes 14680064 | tf_op jit(solution)/shard_map/all_to_all | solution.py:33
  462.5 94.0 %all-to-all-done.3 = bf16[64,6,7168]{2,1,0:T(8,128)(2,1)} async-done(((bf16[64,6,7168]{2,1,0:T(8,128)(2,1)}), bf16[64,6,7168]{2,1,0:T(8,128)(2,1)}, u32[]{:S(2)}, u32[]{:S(2)}) %all-to-all-start.3) | async-done | bytes 5505056 | tf_op jit(solution)/shard_map/all_to_all | solution.py:33
  556.5 7.8 %bitcast_reduce_fusion = bf16[32,6,7168]{2,1,0:T(8,128)(2,1)} fusion(bf16[64,6,7168]{2,1,0:T(8,128)(2,1)} %all-to-all-done.3), kind=kLoop, calls=%fused_computation.8 | loop fusion | flops 1376256 | bytes 8257536 | tf_op jit(solution)/shard_map/reduce_sum | solution.py:66
  564.4 3.2 reshape.205
  567.6 3.0 gather_fusion.3
  570.5 5.3 reshape.208
  575.8 7.1 %multiply_reduce_fusion = f32[64,7168]{1,0:T(8,128)S(1)} fusion(f32[64,2,7168]{2,1,0:T(2,128)} %reshape.208, f32[64,2]{1,0:T(8,128)S(1)} %copy.17), kind=kLoop, calls=%fused_computation.20 | loop fusion | flops 1376256 | bytes 5505536 | tf_op jit(solution)/shard_map/reduce_sum | solution.py:70
  (52 shorter events, 8.1 us)
Async XLA Ops:
  155.8 7.5 %copy-start.4 = (f32[1,2,64,2]{2,3,1,0:T(2,128)S(1)}, f32[1,2,64,2]{2,3,1,0:T(2,128)}, u32[]{:S(2)}) copy-start(f32[1,2,64,2]{2,3,1,0:T(2,128)} %param.10) | copy-start | bytes 3076
  155.8 101.6 %all-to-all-start.1 = ((bf16[64,6,7168]{2,1,0:T(8,128)(2,1)}), bf16[64,6,7168]{2,1,0:T(8,128)(2,1)}, u32[]{:S(2)}, u32[]{:S(2)}) async-start(bf16[64,6,7168]{2,1,0:T(8,128)(2,1)} %reshape.197), calls=%async_computation.1 | async-start | bytes 14680064 | tf_op jit(solution)/shard_map/all_to_all | solution.py:33
  271.5 12.4 %copy-start = (bf16[1,64,7168]{2,1,0:T(8,128)(2,1)S(1)}, bf16[1,64,7168]{2,1,0:T(8,128)(2,1)}, u32[]{:S(2)}) copy-start(bf16[1,64,7168]{2,1,0:T(8,128)(2,1)} %param.7) | copy-start | bytes 2752516
  276.8 27.4 %copy-start.3 = (f32[1,7168]{1,0:T(1,128)S(1)}, f32[1,7168]{1,0:T(1,128)}, u32[]{:S(2)}) copy-start(f32[1,7168]{1,0:T(1,128)} %param.8) | copy-start | bytes 86020
  284.2 19.1 %collective-permute-start = (bf16[64,7168]{1,0:T(8,128)(2,1)S(1)}, bf16[64,7168]{1,0:T(8,128)(2,1)S(1)}, u32[]{:S(2)}, u32[]{:S(2)}) collective-permute-start(bf16[64,7168]{1,0:T(8,128)(2,1)S(1)} %fusion.17), channel_id=1, source_target_pairs={{0,64},{64,0},{1,65},{65,1},{2,66},{66,2},{3,67},{67,3},{4,68},{68... | collective-permute-start | bytes 2752520 | tf_op jit(solution)/shard_map/ppermute | solution.py:15
  303.3 0.9 copy-start.1
  454.9 101.6 %all-to-all-start.3 = ((bf16[64,6,7168]{2,1,0:T(8,128)(2,1)}), bf16[64,6,7168]{2,1,0:T(8,128)(2,1)}, u32[]{:S(2)}, u32[]{:S(2)}) async-start(bf16[64,6,7168]{2,1,0:T(8,128)(2,1)} %reshape.203), calls=%async_computation.3 | async-start | bytes 14680064 | tf_op jit(solution)/shard_map/all_to_all | solution.py:33
  570.5 12.4 %copy-start.2 = (bf16[64,7168]{1,0:T(8,128)(2,1)S(1)}, bf16[64,7168]{1,0:T(8,128)(2,1)}, u32[]{:S(2)}) copy-start(bf16[64,7168]{1,0:T(8,128)(2,1)} %copy-done.1) | copy-start | bytes 2752516
where the time goes:
time: 595 us; the launch traced here: 584 us
  waiting for transfers between devices  203 us (34%)
  blocking collectives  192 us (32%)
  local copies, waits for them, and re-layouts  90.8 us (15%)
  matrix products  44.1 us (7%)
  other arithmetic  36.4 us (6%)
  starting transfers between devices  17.9 us (3%)
    all_to_all x2, blocking collectives, expert_block(): lax.all_to_all(outgoing, 'ep', split_axis=0, concat_axis=0, tiled=True)  192 us
    all_to_all x2, waiting for transfers between devices, return_partials(): lax.all_to_all(partial_value, 'ep', split_axis=0, concat_axis=0, tiled=True)  188 us
    dot_general x2, matrix products, expert_rows(): jnp.dot(hidden, w_down, preferred_element_type=jnp.float32)  30.2 us
    gather x4, local copies, waits for them, and re-layouts, expert_block(): outgoing = padded[sources]  29.6 us
    reshape x2, local copies, waits for them, and re-layouts, expert_rows(): stacked = received.reshape(-1, width)  17.1 us
    reshape x2, local copies, waits for them, and re-layouts, expert_rows(): return partial_value.reshape(received.shape)  16.7 us
    reduce_sum x2, other arithmetic, expert_block(): returned.reshape(experts, SHARDS, capacity, width).astype(jnp.float32)  15.7 us
    all_to_all x2, starting transfers between devices, return_partials(): lax.all_to_all(partial_value, 'ep', split_axis=0, concat_axis=0, tiled=True)  15 us
  transfers between devices with their start and end apart: 3, of which 3 were waited for; matrix products, arithmetic and copies ran while one was open for 0% of the time, Pallas kernels for 0%

commit v1 on v0

v1 whole, which is shorter than its diff:
```python
import functools

import jax
import jax.numpy as jnp
import numpy as np
from jax import lax
from jax.experimental import pallas as pl
from jax.experimental.pallas import tpu as pltpu
from jax.sharding import PartitionSpec as P

EPS = 1e-06
SLOTS = 6
PARTS = 4
ROWS = SLOTS * PARTS
GROUP = 8
VMEM = 60 * 1024 * 1024

f32 = jnp.float32
bf16 = jnp.bfloat16


def spec(space=pltpu.VMEM):
    return pl.BlockSpec(memory_space=space)


def to_bf16(condition):
    return jnp.where(condition, 1.0, 0.0).astype(bf16)


def earlier_matrix(tokens):
    size = PARTS * tokens
    a, b = np.arange(size)[:, None], np.arange(size)[None, :]
    return ((a // tokens == b // tokens) & (a % tokens < b % tokens)).astype(jnp.bfloat16)


def order_matrix():
    size = GROUP * ROWS
    out = np.arange(size)
    q, rest = out // (GROUP * SLOTS), out % (GROUP * SLOTS)
    message, slot = rest // SLOTS, rest % SLOTS
    matrix = np.zeros((size, size), jnp.bfloat16)
    matrix[out, message * ROWS + q * SLOTS + slot] = 1
    return matrix


def selection(routes_ref, index, earlier_ref, tokens, experts):
    rows, columns = experts * ROWS, PARTS * tokens
    token = lax.broadcasted_iota(jnp.int32, (tokens, columns), 0)
    column = lax.broadcasted_iota(jnp.int32, (tokens, columns), 1)
    spread = to_bf16(token == lax.rem(column, tokens))
    chosen = routes_ref[index].astype(f32).astype(bf16)
    chosen = jnp.dot(chosen, spread, preferred_element_type=f32).astype(jnp.int32)
    row = lax.broadcasted_iota(jnp.int32, (rows, columns), 0)
    expert = lax.div(row, ROWS)
    rest = row - expert * ROWS
    piece = lax.div(rest, SLOTS)
    slot = rest - piece * SLOTS
    first = expert == chosen[0:1, :]
    named = jnp.logical_or(first, expert == chosen[1:2, :])
    before = jnp.dot(to_bf16(named), earlier_ref[...], preferred_element_type=f32)
    own = lax.div(lax.broadcasted_iota(jnp.int32, (rows, columns), 1), tokens)
    fits = jnp.logical_and(before.astype(jnp.int32) == slot, piece == own)
    return jnp.logical_and(named, fits), first


def put_normed(tokens_ref, gain_ref, stack_ref):
    tokens, width = tokens_ref.shape
    part = width // PARTS
    total = jnp.zeros((tokens, 1), f32)
    for q in range(PARTS):
        piece = tokens_ref[:, q * part : (q + 1) * part].astype(f32)
        total += jnp.sum(piece * piece, axis=1, keepdims=True)
    inverse = lax.rsqrt(total / width + EPS)
    for q in range(PARTS):
        piece = tokens_ref[:, q * part : (q + 1) * part].astype(f32)
        normed = piece * inverse * gain_ref[:, q * part : (q + 1) * part]
        stack_ref[q * tokens : (q + 1) * tokens, :] = normed.astype(bf16)


def put_packed(matrix, stack_ref, out_ref):
    out_ref[...] = jnp.dot(matrix, stack_ref[...], preferred_element_type=f32).astype(bf16)


def first_pack(experts, index_ref, tokens_ref, gain_ref, routes_ref, earlier_ref, out_ref, stack_ref):
    fills, _ = selection(routes_ref, index_ref[0], earlier_ref, tokens_ref.shape[0], experts)
    put_normed(tokens_ref, gain_ref, stack_ref)
    put_packed(to_bf16(fills), stack_ref, out_ref)


def second_pack(tokens_ref, gain_ref, send_ref, out_ref, stack_ref):
    put_normed(tokens_ref, gain_ref, stack_ref)
    put_packed(send_ref[...], stack_ref, out_ref)


def routing(experts, tokens, index_ref, routes_ref, gates_ref, earlier_ref, send_ref, *weights_refs):
    columns = PARTS * tokens
    token = lax.broadcasted_iota(jnp.int32, (tokens, columns), 0)
    column = lax.broadcasted_iota(jnp.int32, (tokens, columns), 1)
    spread = jnp.where(token == lax.rem(column, tokens), 1.0, 0.0)
    for stage in range(2):
        index = index_ref[stage]
        fills, first = selection(routes_ref, index, earlier_ref, tokens, experts)
        if stage == 1:
            send_ref[...] = to_bf16(fills)
        gates = jnp.dot(
            gates_ref[index], spread, preferred_element_type=f32, precision=lax.Precision.HIGHEST
        )
        scaled = jnp.where(fills, jnp.where(first, gates[0:1, :], gates[1:2, :]), 0.0).T
        high = scaled.astype(bf16)
        weights_refs[stage][0] = high
        weights_refs[stage][1] = (scaled - high.astype(f32)).astype(bf16)


def combine(tokens_ref, weights_ref, returned_ref, out_ref):
    tokens, width = tokens_ref.shape
    part = width // PARTS
    returned = returned_ref[...]
    for q in range(PARTS):
        rows = slice(q * tokens, (q + 1) * tokens)
        added = jnp.dot(weights_ref[0, rows, :], returned, preferred_element_type=f32)
        added += jnp.dot(weights_ref[1, rows, :], returned, preferred_element_type=f32)
        columns = slice(q * part, (q + 1) * part)
        out_ref[:, columns] = (tokens_ref[:, columns].astype(f32) + added).astype(bf16)


DEPTH = 3


def experts_kernel(
    arrived_ref, order_ref, back_ref, g0, u0, d0, g1, u1, d1, out_ref,
    stack_ref, first_buf, second_buf, act_ref, hidden_ref, result_ref, first_sem, second_sem,
):
    rows = stack_ref.shape[1]
    part = stack_ref.shape[2]
    half = g0.shape[1]
    groups = rows // (GROUP * SLOTS)
    size = GROUP * ROWS
    take = GROUP * SLOTS
    steps = [(gate, up, q) for gate, up in ((g0, u0), (g1, u1)) for q in range(PARTS)]

    def load_first(step):
        gate, up, q = steps[step]
        slot = step % DEPTH
        lines = pl.ds(q * part, part)
        return [
            pltpu.make_async_copy(
                source.at[lines, :], first_buf.at[slot, :, pl.ds(i * half, half)], first_sem.at[slot, i]
            )
            for i, source in enumerate((gate, up))
        ]

    def load_second(q):
        return [
            pltpu.make_async_copy(
                source.at[:, pl.ds(q * part, part)],
                second_buf.at[q, pl.ds(i * half, half), :],
                second_sem.at[q, i],
            )
            for i, source in enumerate((d0, d1))
        ]

    def start(copies):
        for copy in copies:
            copy.start()

    def wait(copies):
        for copy in copies:
            copy.wait()

    for step in range(DEPTH):
        start(load_first(step))
    for group in range(groups):
        moved = jnp.dot(
            order_ref[...], arrived_ref[group * size : (group + 1) * size, :], preferred_element_type=f32
        ).astype(bf16)
        for q in range(PARTS):
            stack_ref[q, group * take : (group + 1) * take, :] = moved[q * take : (q + 1) * take, :]
    for step in range(len(steps)):
        q = step % PARTS
        wait(load_first(step))
        product = jnp.dot(stack_ref[q], first_buf[step % DEPTH], preferred_element_type=f32)
        if q == 0:
            act_ref[...] = product
        else:
            act_ref[...] += product
        if step + DEPTH < len(steps):
            start(load_first(step + DEPTH))
        if step >= len(steps) - PARTS:
            start(load_second(step - len(steps) + PARTS))
        if q == PARTS - 1:
            gate = act_ref[:, :half]
            value = gate / (1.0 + jnp.exp(-gate)) * act_ref[:, half:]
            at = (step // PARTS) * half
            hidden_ref[:, at : at + half] = value.astype(bf16)
    for q in range(PARTS):
        wait(load_second(q))
        product = jnp.dot(hidden_ref[...], second_buf[q], preferred_element_type=f32).astype(bf16)
        for group in range(groups):
            result_ref[group, q * take : (q + 1) * take, :] = product[group * take : (group + 1) * take, :]
    for group in range(groups):
        out_ref[group * size : (group + 1) * size, :] = jnp.dot(
            back_ref[...], result_ref[group], preferred_element_type=f32
        ).astype(bf16)


def shards(entering, norm_gain, routes, route_gates, w_gate, w_up, w_down):
    section = lax.axis_index("pp")
    devices = lax.axis_size("ep")
    chips = devices // 2
    experts = chips
    own = entering[0]
    tokens, width = own.shape
    part = width // PARTS
    half = w_gate.shape[2]
    gain = norm_gain
    chosen = jnp.swapaxes(routes[0], 1, 2)
    gates = jnp.swapaxes(route_gates[0], 1, 2)
    order_of = jnp.stack([section, 1 - section]).astype(jnp.int32)
    earlier = jnp.asarray(earlier_matrix(tokens))
    order = order_matrix()
    forth, back = jnp.asarray(order), jnp.asarray(order.T)
    same_core = [[2 * chip + core for chip in range(chips)] for core in range(2)]
    cores = [(device, device ^ 1) for device in range(devices)]
    message_rows = experts * ROWS
    received_rows = chips * SLOTS

    other = [lax.ppermute(w[0], "ep", cores) for w in (w_gate, w_up, w_down)]
    mine = [w[0] for w in (w_gate, w_up, w_down)]

    params = pltpu.CompilerParams(vmem_limit_bytes=VMEM)

    def cost(flops, size):
        return pl.CostEstimate(flops=flops, bytes_accessed=size, transcendentals=0)

    packed_shape = jax.ShapeDtypeStruct((message_rows, part), bf16)
    stack = pltpu.VMEM((PARTS * tokens, part), bf16)
    pack_cost = cost(2 * message_rows * PARTS * tokens * part, 4 * tokens * width * 2)

    def exchange(rows):
        return lax.all_to_all(
            rows, "ep", split_axis=0, concat_axis=0, tiled=True, axis_index_groups=same_core
        )

    def run_experts(arrived):
        return pl.pallas_call(
            experts_kernel,
            out_shape=packed_shape,
            in_specs=[spec()] * 3 + [spec(pl.ANY)] * 6,
            out_specs=spec(),
            scratch_shapes=[
                pltpu.VMEM((PARTS, received_rows, part), bf16),
                pltpu.VMEM((DEPTH, part, 2 * half), bf16),
                pltpu.VMEM((PARTS, 2 * half, part), bf16),
                pltpu.VMEM((received_rows, 2 * half), f32),
                pltpu.VMEM((received_rows, 2 * half), bf16),
                pltpu.VMEM((received_rows // (GROUP * SLOTS), GROUP * ROWS, part), bf16),
                pltpu.SemaphoreType.DMA((DEPTH, 2)),
                pltpu.SemaphoreType.DMA((PARTS, 2)),
            ],
            compiler_params=params,
            cost_estimate=cost(12 * received_rows * width * half, 12 * width * half),
            name="experts",
        )(arrived, forth, back, *mine, *other)

    def run_combine(rows, weights, returned):
        return pl.pallas_call(
            combine,
            out_shape=jax.ShapeDtypeStruct((tokens, width), bf16),
            in_specs=[spec()] * 3,
            out_specs=spec(),
            compiler_params=params,
            cost_estimate=cost(4 * message_rows * PARTS * tokens * part, 5 * tokens * width * 2),
            name="combine",
        )(rows, weights, returned)

    packed = pl.pallas_call(
        functools.partial(first_pack, experts),
        out_shape=packed_shape,
        in_specs=[spec(pltpu.SMEM)] + [spec()] * 4,
        out_specs=spec(),
        scratch_shapes=[stack],
        compiler_params=params,
        cost_estimate=pack_cost,
        name="first_pack",
    )(order_of, own, gain, chosen, earlier)
    weights_shape = jax.ShapeDtypeStruct((2, PARTS * tokens, message_rows), bf16)
    send, first_weights, second_weights = pl.pallas_call(
        functools.partial(routing, experts, tokens),
        out_shape=(
            jax.ShapeDtypeStruct((message_rows, PARTS * tokens), bf16),
            weights_shape,
            weights_shape,
        ),
        in_specs=[spec(pltpu.SMEM)] + [spec()] * 3,
        out_specs=(spec(), spec(), spec()),
        compiler_params=params,
        cost_estimate=cost(message_rows * PARTS * tokens * 1000, 3 * message_rows * PARTS * tokens * 2),
        name="routing",
    )(order_of, chosen, gates, earlier)

    moved = run_combine(own, first_weights, exchange(run_experts(exchange(packed))))
    arrived = lax.ppermute(moved, "pp", [(0, 1), (1, 0)])
    packed = pl.pallas_call(
        second_pack,
        out_shape=packed_shape,
        in_specs=[spec()] * 3,
        out_specs=spec(),
        scratch_shapes=[stack],
        compiler_params=params,
        cost_estimate=pack_cost,
        name="second_pack",
    )(arrived, gain, send)
    finished = run_combine(arrived, second_weights, exchange(run_experts(exchange(packed))))
    return finished[None]


def solution(mesh):
    return jax.shard_map(
        shards,
        mesh=mesh,
        in_specs=(
            P("pp", "ep", None),
            P("pp", None),
            P("pp", None, "ep", None),
            P("pp", None, "ep", None),
            P("pp", None, "ep"),
            P("pp", None, "ep"),
            P("pp", "ep", None),
        ),
        out_specs=P("pp", "ep", None),
        check_vma=False,
    )
```

time: 595 us -> 254 us (0.43); the launches traced: 584 us -> 253 us
  waiting for transfers between devices: 203 us -> 50.4 us
  local copies, waits for them, and re-layouts: 90.8 us -> 2.44 us
  blocking collectives: 192 us -> 126 us
  Pallas kernels: 0 us -> 65.5 us
  matrix products: 44.1 us -> 0 us
  other arithmetic: 36.4 us -> 0.57 us
  starting transfers between devices: 17.9 us -> 8.26 us
    all_to_all x2 -> x1, waiting for transfers between devices: 188 us -> 32 us  [exchange(): lax.all_to_all(rows, 'ep', split_axis=0, concat_axis=0, tiled=True, axis_...]
    all_to_all x2 -> x3, blocking collectives: 192 us -> 126 us  [exchange(): lax.all_to_all(rows, 'ep', split_axis=0, concat_axis=0, tiled=True, axis_...]
    pallas_call x0 -> x7, Pallas kernels: none -> 65.5 us  [the longest x2 39.6 us: run_experts(): pl.pallas_call(experts_kernel, out_shape=packed_shape, in_specs=[spec()]...]
    dot_general x4 -> x0, matrix products: 44.1 us -> none  [the longest x2 30.2 us: expert_rows(): jnp.dot(hidden, w_down, preferred_element_type=jnp.float32)]
    reshape x8 -> x0, local copies, waits for them, and re-layouts: 40.4 us -> none  [the longest x2 17.1 us: expert_rows(): stacked = received.reshape(-1, width)]
    gather x6 -> x0, local copies, waits for them, and re-layouts: 35.5 us -> none  [the longest x4 29.6 us: expert_block(): outgoing = padded[sources]]
    reduce_sum x8 -> x0, other arithmetic: 32 us -> none  [the longest x2 15.7 us: expert_block(): returned.reshape(experts, SHARDS, capacity, width).astype(jnp.float32)]
    convert_element_type x2 -> x0, local copies, waits for them, and re-layouts: 10.6 us -> none  [expert_block(): summed[position].astype(jnp.float32).reshape(token_count, topk, width)]
  transfers between devices with their start and end apart: 3 -> 5, of which waited for: 3 -> 2; matrix products, arithmetic and copies ran while one was open for 0% -> 0% of each run, Pallas kernels for 0% -> 3%
where the time goes in v1:
time: 254 us; the launch traced here: 253 us
  blocking collectives  126 us (50%)
  Pallas kernels  65.5 us (26%)
  waiting for transfers between devices  50.4 us (20%)
  starting transfers between devices  8.26 us (3%)
    all_to_all x3, blocking collectives, exchange(): lax.all_to_all(rows, 'ep', split_axis=0, concat_axis=0, tiled=True, axis_...  126 us
    pallas_call x2, Pallas kernels, run_experts(): pl.pallas_call(experts_kernel, out_shape=packed_shape, in_specs=[spec()]...  39.6 us
    all_to_all x1, waiting for transfers between devices, exchange(): lax.all_to_all(rows, 'ep', split_axis=0, concat_axis=0, tiled=True, axis_...  32 us
    ppermute x1, waiting for transfers between devices, shards(): arrived = lax.ppermute(moved, 'pp', [(0, 1), (1, 0)])  18.4 us
    pallas_call x2, Pallas kernels, run_combine(): pl.pallas_call(combine, out_shape=jax.ShapeDtypeStruct((tokens, width), b...  14.3 us
  transfers between devices with their start and end apart: 5, of which 2 were waited for; matrix products, arithmetic and copies ran while one was open for 0% of the time, Pallas kernels for 3%

profile of v1, /device:TPU:0, one launch (start us, length us, event | category | flops | bytes accessed | tf_op | source)
XLA Modules:
  0.0 253.1 jit_solution(10072198711128506970)
XLA Ops:
  0.0 0.0 collective-permute-start
  0.0 0.5 collective-permute-start.1
  0.5 0.0 collective-permute-start.2
  0.5 0.6 pad_add_fusion.index_ref
  1.1 4.3 %first_pack.1 = bf16[768,1792]{1,0:T(8,128)(2,1)} custom-call(s32[2]{0:T(128)} %pad_add_fusion.index_ref, bf16[64,7168]{1,0:T(8,128)(2,1)} %bitcast.38, f32[1,7168]{1,0:T(1,128)} %gain_ref.3, s32[2,2,64]{2,1,0:T(2,128)} %bitcast.40, bf16[256,256]{1,0:T(8,128)(2,1)} %constant.14.clone.earlier_ref), custom_call_target="tpu_custom_call" | custom-call | flops 704643072 | bytes 3670016 | tf_op jit(solution)/shard_map/first_pack/pallas_call | solution.py:276
  5.4 45.1 %all_to_all.44 = bf16[32,24,1792]{2,1,0:T(8,128)(2,1)} all-to-all(bf16[32,24,1792]{2,1,0:T(8,128)(2,1)} %bitcast.31), channel_id=1, replica_groups={{0,2,4,6,8,10,12,14,16,18,20,22,24,26,28,30,32,34,36,38,40,42,44,46,48,..., dimensions={0} | all-to-all | bytes 5505024 | tf_op jit(solution)/shard_map/all_to_all | solution.py:240
  50.4 0.0 collective-permute-done.g1
  50.4 0.0 collective-permute-done.1.u1
  50.4 0.0 collective-permute-done.2.d1
  50.5 19.7 %experts.2 = bf16[768,1792]{1,0:T(8,128)(2,1)} custom-call(bf16[768,1792]{1,0:T(8,128)(2,1)} %bitcast.35, bf16[192,192]{1,0:T(8,128)(2,1)} %constant.15.clone.order_ref, bf16[192,192]{1,0:T(8,128)(2,1)} %constant.16.clone.back_ref, bf16[7168,512]{1,0:T(8,128)(2,1)} %bitcast.22, bf16[7168,512]{1,0:T(8,128)(2,1)} %bitcast.25, bf16[512,7168]{1,0:T(8,128)(2,1)} %bitcast.28, ...), custom_call_target="tpu_custom_call" | custom-call | flops 8455716864 | bytes 44040192 | tf_op jit(solution)/shard_map/experts/pallas_call | solution.py:245
  70.2 4.8 %all-to-all-start.1 = ((bf16[32,24,1792]{2,1,0:T(8,128)(2,1)}), bf16[32,24,1792]{2,1,0:T(8,128)(2,1)S(1)}, u32[]{:S(2)}, u32[]{:S(2)}) async-start(bf16[32,24,1792]{2,1,0:T(8,128)(2,1)} %bitcast.34), calls=%async_computation.1 | async-start | bytes 5505024 | tf_op jit(solution)/shard_map/all_to_all | solution.py:240
  75.1 3.3 %routing.1 = (bf16[768,256]{1,0:T(8,128)(2,1)}, bf16[2,256,768]{2,1,0:T(8,128)(2,1)}, bf16[2,256,768]{2,1,0:T(8,128)(2,1)}) custom-call(s32[2]{0:T(128)} %pad_add_fusion.index_ref, s32[2,2,64]{2,1,0:T(2,128)} %bitcast.41, f32[2,2,64]{2,1,0:T(2,128)} %bitcast.42, bf16[256,256]{1,0:T(8,128)(2,1)} %constant.14.clone.earlier_ref), custom_call_target="tpu_custom_call" | custom-call | flops 196608000 | bytes 1179648 | tf_op jit(solution)/shard_map/routing/pallas_call | solution.py:287
  78.4 32.0 %all-to-all-done.1 = bf16[32,24,1792]{2,1,0:T(8,128)(2,1)S(1)} async-done(((bf16[32,24,1792]{2,1,0:T(8,128)(2,1)}), bf16[32,24,1792]{2,1,0:T(8,128)(2,1)S(1)}, u32[]{:S(2)}, u32[]{:S(2)}) %all-to-all-start.1) | async-done | bytes 2752544 | tf_op jit(solution)/shard_map/all_to_all | solution.py:240
  110.3 0.0 copy-start
  110.3 1.5 copy-done
  111.8 7.1 %combine.2 = bf16[64,7168]{1,0:T(8,128)(2,1)} custom-call(bf16[64,7168]{1,0:T(8,128)(2,1)} %bitcast.39, bf16[2,256,768]{2,1,0:T(8,128)(2,1)} %get-tuple-element.8.weights_ref, bf16[768,1792]{1,0:T(8,128)(2,1)} %bitcast.32), custom_call_target="tpu_custom_call" | custom-call | flops 1409286144 | bytes 4587520 | tf_op jit(solution)/shard_map/combine/pallas_call | solution.py:266
  119.0 2.9 %collective-permute-start.3 = (bf16[64,7168]{1,0:T(8,128)(2,1)}, bf16[64,7168]{1,0:T(8,128)(2,1)S(1)}, u32[]{:S(2)}, u32[]{:S(2)}) collective-permute-start(bf16[64,7168]{1,0:T(8,128)(2,1)} %combine.2), channel_id=1, source_target_pairs={{0,64},{64,0},{1,65},{65,1},{2,66},{66,2},{3,67},{67,3},{4,68},{68... | collective-permute-start | bytes 2752520 | tf_op jit(solution)/shard_map/ppermute | solution.py:302
  121.9 18.4 %collective-permute-done.3.tokens_ref = bf16[64,7168]{1,0:T(8,128)(2,1)S(1)} collective-permute-done((bf16[64,7168]{1,0:T(8,128)(2,1)}, bf16[64,7168]{1,0:T(8,128)(2,1)S(1)}, u32[]{:S(2)}, u32[]{:S(2)}) %collective-permute-start.3) | collective-permute-done | bytes 917536 | tf_op jit(solution)/shard_map/ppermute | solution.py:302
  140.3 0.0 copy-start.1
  140.3 0.9 copy-done.1
  141.2 4.1 %second_pack.1 = bf16[768,1792]{1,0:T(8,128)(2,1)} custom-call(bf16[64,7168]{1,0:T(8,128)(2,1)} %copy-done.1, f32[1,7168]{1,0:T(1,128)} %gain_ref.3, bf16[768,256]{1,0:T(8,128)(2,1)} %get-tuple-element.10.send_ref), custom_call_target="tpu_custom_call" | custom-call | flops 704643072 | bytes 3670016 | tf_op jit(solution)/shard_map/second_pack/pallas_call | solution.py:303
  145.3 41.2 %all_to_all.45 = bf16[32,24,1792]{2,1,0:T(8,128)(2,1)} all-to-all(bf16[32,24,1792]{2,1,0:T(8,128)(2,1)} %bitcast.30), channel_id=1, replica_groups={{0,2,4,6,8,10,12,14,16,18,20,22,24,26,28,30,32,34,36,38,40,42,44,46,48,..., dimensions={0} | all-to-all | bytes 5505024 | tf_op jit(solution)/shard_map/all_to_all | solution.py:240
  186.5 19.9 %experts.3 = bf16[768,1792]{1,0:T(8,128)(2,1)} custom-call(bf16[768,1792]{1,0:T(8,128)(2,1)} %bitcast.36, bf16[192,192]{1,0:T(8,128)(2,1)} %constant.15.clone.order_ref, bf16[192,192]{1,0:T(8,128)(2,1)} %constant.16.clone.back_ref, bf16[7168,512]{1,0:T(8,128)(2,1)} %bitcast.23, bf16[7168,512]{1,0:T(8,128)(2,1)} %bitcast.26, bf16[512,7168]{1,0:T(8,128)(2,1)} %bitcast.29, ...), custom_call_target="tpu_custom_call" | custom-call | flops 8455716864 | bytes 44040192 | tf_op jit(solution)/shard_map/experts/pallas_call | solution.py:245
  206.4 39.6 %all_to_all.46 = bf16[32,24,1792]{2,1,0:T(8,128)(2,1)} all-to-all(bf16[32,24,1792]{2,1,0:T(8,128)(2,1)} %bitcast.37), channel_id=1, replica_groups={{0,2,4,6,8,10,12,14,16,18,20,22,24,26,28,30,32,34,36,38,40,42,44,46,48,..., dimensions={0} | all-to-all | bytes 5505024 | tf_op jit(solution)/shard_map/all_to_all | solution.py:240
  246.0 7.1 %combine.3 = bf16[64,7168]{1,0:T(8,128)(2,1)} custom-call(bf16[64,7168]{1,0:T(8,128)(2,1)} %copy-done.1, bf16[2,256,768]{2,1,0:T(8,128)(2,1)} %get-tuple-element.9.weights_ref, bf16[768,1792]{1,0:T(8,128)(2,1)} %bitcast.33), custom_call_target="tpu_custom_call" | custom-call | flops 1409286144 | bytes 4587520 | tf_op jit(solution)/shard_map/combine/pallas_call | solution.py:266
Async XLA Ops:
  0.0 50.4 %collective-permute-start = (bf16[7168,512]{1,0:T(8,128)(2,1)}, bf16[7168,512]{1,0:T(8,128)(2,1)}, u32[]{:S(2)}, u32[]{:S(2)}) collective-permute-start(bf16[7168,512]{1,0:T(8,128)(2,1)} %bitcast.21), channel_id=1, source_target_pairs={{0,1},{1,0},{2,3},{3,2},{4,5},{5,4},{6,7},{7,6},{8,9},{9,8},{10,11... | collective-permute-start | bytes 22020104 | tf_op jit(solution)/shard_map/ppermute | solution.py:227
  0.0 50.4 %collective-permute-start.1 = (bf16[7168,512]{1,0:T(8,128)(2,1)}, bf16[7168,512]{1,0:T(8,128)(2,1)}, u32[]{:S(2)}, u32[]{:S(2)}) collective-permute-start(bf16[7168,512]{1,0:T(8,128)(2,1)} %bitcast.24), channel_id=1, source_target_pairs={{0,1},{1,0},{2,3},{3,2},{4,5},{5,4},{6,7},{7,6},{8,9},{9,8},{10,11... | collective-permute-start | bytes 22020104 | tf_op jit(solution)/shard_map/ppermute | solution.py:227
  0.5 49.9 %collective-permute-start.2 = (bf16[512,7168]{1,0:T(8,128)(2,1)}, bf16[512,7168]{1,0:T(8,128)(2,1)}, u32[]{:S(2)}, u32[]{:S(2)}) collective-permute-start(bf16[512,7168]{1,0:T(8,128)(2,1)} %bitcast.27), channel_id=1, source_target_pairs={{0,1},{1,0},{2,3},{3,2},{4,5},{5,4},{6,7},{7,6},{8,9},{9,8},{10,11... | collective-permute-start | bytes 22020104 | tf_op jit(solution)/shard_map/ppermute | solution.py:227
  70.2 40.1 %all-to-all-start.1 = ((bf16[32,24,1792]{2,1,0:T(8,128)(2,1)}), bf16[32,24,1792]{2,1,0:T(8,128)(2,1)S(1)}, u32[]{:S(2)}, u32[]{:S(2)}) async-start(bf16[32,24,1792]{2,1,0:T(8,128)(2,1)} %bitcast.34), calls=%async_computation.1 | async-start | bytes 5505024 | tf_op jit(solution)/shard_map/all_to_all | solution.py:240
  110.3 1.5 copy-start
  119.0 21.3 %collective-permute-start.3 = (bf16[64,7168]{1,0:T(8,128)(2,1)}, bf16[64,7168]{1,0:T(8,128)(2,1)S(1)}, u32[]{:S(2)}, u32[]{:S(2)}) collective-permute-start(bf16[64,7168]{1,0:T(8,128)(2,1)} %combine.2), channel_id=1, source_target_pairs={{0,64},{64,0},{1,65},{65,1},{2,66},{66,2},{3,67},{67,3},{4,68},{68... | collective-permute-start | bytes 2752520 | tf_op jit(solution)/shard_map/ppermute | solution.py:302
  140.3 0.9 copy-start.1

commit v2 on v0

v2 whole, which is shorter than its diff:
```python
import functools

import jax
import jax.numpy as jnp
import numpy as np
from jax import lax
from jax.experimental import pallas as pl
from jax.experimental.pallas import tpu as pltpu
from jax.sharding import PartitionSpec as P

EPS = 1e-06
SLOTS = 6
PARTS = 4
ROWS = SLOTS * PARTS
GROUP = 8
TAKE = GROUP * SLOTS
SIZE = GROUP * ROWS
AHEAD = 1
AHEAD_FLOPS = 20_000_000_000
INFO = 16
MIB = 1024 * 1024

f32 = jnp.float32
bf16 = jnp.bfloat16


def spec(space=pltpu.VMEM):
    return pl.BlockSpec(memory_space=space)


def to_bf16(condition):
    return jnp.where(condition, 1.0, 0.0).astype(bf16)


def earlier_matrix(tokens):
    size = PARTS * tokens
    a, b = np.arange(size)[:, None], np.arange(size)[None, :]
    return ((a // tokens == b // tokens) & (a % tokens < b % tokens)).astype(jnp.bfloat16)


def order_matrix():
    out = np.arange(SIZE)
    q, rest = out // TAKE, out % TAKE
    message, slot = rest // SLOTS, rest % SLOTS
    matrix = np.zeros((SIZE, SIZE), jnp.bfloat16)
    matrix[out, message * ROWS + q * SLOTS + slot] = 1
    return matrix


def spread_matrix(tokens):
    columns = np.arange(PARTS * tokens)
    return (np.arange(tokens)[:, None] == columns[None, :] % tokens).astype(np.float32)


def selection(routes, spread_ref, earlier_ref, tokens, experts):
    rows, columns = experts * ROWS, PARTS * tokens
    chosen = jnp.dot(routes, spread_ref[...], preferred_element_type=f32, precision=lax.Precision.HIGHEST)
    chosen = chosen.astype(jnp.int32)
    row = lax.broadcasted_iota(jnp.int32, (rows, 128), 0)
    expert = (row * 2731) >> 16
    rest = row - expert * ROWS
    piece = (rest * 43) >> 8
    slot = rest - piece * SLOTS
    wide = columns // 128
    expert, slot, piece = (jnp.concatenate([x] * wide, axis=1) for x in (expert, slot, piece))
    first = expert == chosen[0:1, :]
    named = jnp.logical_or(first, expert == chosen[1:2, :])
    before = jnp.dot(to_bf16(named), earlier_ref[...], preferred_element_type=f32)
    own = lax.broadcasted_iota(jnp.int32, (rows, columns), 1) // tokens
    fits = jnp.logical_and(before.astype(jnp.int32) == slot, piece == own)
    return jnp.logical_and(named, fits), first


def first_pack(
    experts, section_ref, tokens_ref, routes_ref, gates_ref, spread_ref, earlier_ref, out_ref, cross_ref, stack_ref
):
    tokens, width = tokens_ref.shape
    part = width // PARTS
    cross_ref[:tokens, :] = tokens_ref[:, width // 2 :]
    cross_ref[tokens:, :] = jnp.zeros((INFO, width // 2), bf16)
    rest = jnp.concatenate([gates_ref[0], gates_ref[1]], axis=0)
    info = [jnp.concatenate([routes_ref[0], routes_ref[1]], axis=0).astype(f32)]
    for _ in range(3):
        term = rest.astype(bf16).astype(f32)
        info.append(term)
        rest = rest - term
    cross_ref[tokens:, :tokens] = jnp.concatenate(info, axis=0).astype(bf16)
    routes = routes_ref[section_ref[0]].astype(f32)
    fills, _ = selection(routes, spread_ref, earlier_ref, tokens, experts)
    for q in range(PARTS):
        stack_ref[q * tokens : (q + 1) * tokens, :] = tokens_ref[:, q * part : (q + 1) * part]
    out_ref[...] = jnp.dot(to_bf16(fills), stack_ref[...], preferred_element_type=f32).astype(bf16)


def routing(
    experts, tokens, section_ref, own_routes, own_gates, cross_ref, spread_ref, earlier_ref,
    send_ref, first_ref, last_ref,
):
    section = section_ref[0]
    columns = PARTS * tokens

    info = cross_ref[:, :tokens].astype(f32)

    def of_other(micro):
        choices = [jnp.where(micro == 0, info[at : at + 2, :], info[at + 2 : at + 4, :]) for at in range(0, INFO, 4)]
        return choices[0], choices[1] + choices[2] + choices[3]

    def of_own(micro):
        return own_routes[micro].astype(f32), own_gates[micro]

    def put_weights(gates, fills, first, weights_ref, at):
        gates = jnp.dot(gates, spread_ref[...], preferred_element_type=f32, precision=lax.Precision.HIGHEST)
        scaled = jnp.where(fills, jnp.where(first, gates[0:1, :], gates[1:2, :]), 0.0).T
        high = scaled.astype(bf16)
        weights_ref[at, :columns, :] = high
        weights_ref[at, columns:, :] = (scaled - high.astype(f32)).astype(bf16)

    def select(routes):
        return selection(routes, spread_ref, earlier_ref, tokens, experts)

    routes, gates = of_own(section)
    put_weights(gates, *select(routes), first_ref, section)
    routes, gates = of_other(1 - section)
    put_weights(gates, *select(routes), first_ref, 1 - section)
    routes, _ = of_other(section)
    send_ref[1 - section] = to_bf16(select(routes)[0])
    routes, gates = of_own(1 - section)
    fills, first = select(routes)
    send_ref[section] = to_bf16(fills)
    put_weights(gates, fills, first, last_ref, 0)


def add_returned(weights, returned):
    both = jnp.dot(weights, returned, preferred_element_type=f32)
    half = both.shape[0] // 2
    return both[:half, :] + both[half:, :]


def turn(section_ref, own_ref, other_ref, weights_ref, returned_ref, send_ref, out_ref, kept_ref, came_ref, stack_ref):
    section = section_ref[0]
    tokens = own_ref.shape[0]
    lines, part = send_ref.shape[1], returned_ref.shape[1]
    for before_ref, after_ref, start, home, target in (
        (own_ref, kept_ref, 0, section, 1 - section),
        (other_ref, came_ref, 0, 1 - section, section),
    ):
        returned = returned_ref[pl.ds(pl.multiple_of(home * lines, lines), lines), :]
        added = add_returned(weights_ref[home], returned)
        for q in range(PARTS):
            rows, columns = slice(q * tokens, (q + 1) * tokens), slice(start + q * part, start + (q + 1) * part)
            value = (before_ref[:tokens, columns].astype(f32) + added[rows, :]).astype(bf16)
            after_ref[:, q * part : (q + 1) * part] = value
            stack_ref[rows, :] = value
        out_ref[pl.ds(pl.multiple_of(target * lines, lines), lines), :] = jnp.dot(
            send_ref[target], stack_ref[...], preferred_element_type=f32
        ).astype(bf16)


def combine(first_ref, second_ref, weights_ref, returned_ref, out_ref):
    tokens, width = out_ref.shape
    part = width // PARTS
    added = add_returned(weights_ref[0], returned_ref[...])
    for q in range(PARTS):
        source = first_ref if q < PARTS // 2 else second_ref
        at = (q % (PARTS // 2)) * part
        value = source[:, at : at + part].astype(f32) + added[q * tokens : (q + 1) * tokens, :]
        out_ref[:, q * part : (q + 1) * part] = value.astype(bf16)


def experts_kernel(
    crossed, section_ref, arrived_ref, gain_ref, order_ref, back_ref, g0, u0, d0, g1, u1, d1, out_ref,
    stack_ref, first_buf, second_buf, act_ref, hidden_ref, first_sem, second_sem,
):
    section = section_ref[0]
    rows, part = stack_ref.shape[1], stack_ref.shape[2]
    eighth = part // 2
    width = PARTS * part
    half = g0.shape[1]
    groups = rows // TAKE
    lines = groups * SIZE

    def columns_of(q):
        if crossed:
            return pl.ds(q * part, part)
        return pl.ds(pl.multiple_of((jnp.where(section == q // 2, 0, 2) + q % 2) * part, part), part)

    def load_first(q):
        return [
            pltpu.make_async_copy(
                source.at[pl.ds(q * part, part), :],
                first_buf.at[q, :, pl.ds(i * half, half)],
                first_sem.at[q, i],
            )
            for i, source in enumerate((g1, u1))
        ]

    def load_second(q):
        return [pltpu.make_async_copy(d1.at[:, columns_of(q)], second_buf.at[q], second_sem.at[q])]

    queue = [load_first(q) for q in range(PARTS)] + [load_second(q) for q in range(PARTS)]

    def wait(copies):
        for copy in copies:
            copy.wait()

    def start(copies):
        for copy in copies:
            copy.start()

    for copies in queue[:AHEAD]:
        start(copies)

    def wait(copies):
        for copy in copies:
            copy.wait()

    def reorder(at):
        return jnp.dot(order_ref[...], arrived_ref[pl.ds(at, SIZE), :], preferred_element_type=f32)

    def put_normed(at, pieces):
        total = sum(jnp.sum(piece * piece, axis=1, keepdims=True) for piece, _, _, _ in pieces)
        inverse = lax.rsqrt(total / width + EPS)
        for piece, quarter, column, gain in pieces:
            stack_ref[quarter, at : at + TAKE, column : column + piece.shape[1]] = (
                piece * inverse * gain
            ).astype(bf16)

    for group in range(groups):
        pieces = []
        if crossed:
            for side in range(2):
                home = 1 - section if side == 0 else section
                moved = reorder(pl.multiple_of(home * lines + group * SIZE, SIZE))
                for q in range(PARTS):
                    at = (side * PARTS + q) * eighth
                    pieces.append(
                        (moved[q * TAKE : (q + 1) * TAKE, :], 2 * side + q // 2, (q % 2) * eighth,
                         gain_ref[:, at : at + eighth])
                    )
        else:
            moved = reorder(group * SIZE)
            for q in range(PARTS):
                pieces.append(
                    (moved[q * TAKE : (q + 1) * TAKE, :], q, 0, gain_ref[:, q * part : (q + 1) * part])
                )
        put_normed(group * TAKE, pieces)

    def put_hidden(at):
        gate = act_ref[:, :half]
        value = gate / (1.0 + jnp.exp(-gate)) * act_ref[:, half:]
        hidden_ref[:, at : at + half] = value.astype(bf16)

    def add(q, at, product):
        if q == 0:
            act_ref[:, at : at + product.shape[1]] = product
        else:
            act_ref[:, at : at + product.shape[1]] += product

    for q in range(PARTS):
        for i, source in enumerate((g0, u0)):
            weights = source[q * part : (q + 1) * part, :]
            add(q, i * half, jnp.dot(stack_ref[q], weights, preferred_element_type=f32))
        start(queue[AHEAD + q])
    put_hidden(0)
    for q in range(PARTS):
        wait(queue[q])
        if AHEAD + PARTS + q < len(queue):
            start(queue[AHEAD + PARTS + q])
        add(q, 0, jnp.dot(stack_ref[q], first_buf[q], preferred_element_type=f32))
    put_hidden(half)
    for q in range(PARTS):
        wait(queue[PARTS + q])
        product = jnp.dot(hidden_ref[:, :half], d0[:, columns_of(q)], preferred_element_type=f32)
        product += jnp.dot(hidden_ref[:, half:], second_buf[q], preferred_element_type=f32)
        product = product.astype(bf16)
        for group in range(groups):
            piece = product[group * TAKE : (group + 1) * TAKE, :]
            if crossed:
                stack_ref[group, q * TAKE : (q + 1) * TAKE, :] = piece
            else:
                to = (q // 2) * eighth
                for i in range(2):
                    k = 2 * (q % 2) + i
                    stack_ref[group, k * TAKE : (k + 1) * TAKE, to : to + eighth] = piece[
                        :, i * eighth : (i + 1) * eighth
                    ]
        if not crossed and q % 2 == 1:
            to = (q // 2) * eighth
            for group in range(groups):
                at = ((q // 2) * groups + group) * SIZE
                out_ref[at : at + SIZE, :] = jnp.dot(
                    back_ref[...], stack_ref[group, :, to : to + eighth], preferred_element_type=f32
                ).astype(bf16)
    if crossed:
        for group in range(groups):
            out_ref[group * SIZE : (group + 1) * SIZE, :] = jnp.dot(
                back_ref[...], stack_ref[group], preferred_element_type=f32
            ).astype(bf16)


def shards(entering, norm_gain, routes, route_gates, w_gate, w_up, w_down):
    section = lax.axis_index("pp")
    devices = lax.axis_size("ep")
    chips = devices // 2
    experts = chips
    own = entering[0]
    tokens, width = own.shape
    part = width // PARTS
    side = width // 2
    half = w_gate.shape[2]
    lines = experts * ROWS
    received = chips * SLOTS
    columns = PARTS * tokens

    sections = [(0, 1), (1, 0)]
    cores = [(device, device ^ 1) for device in range(devices)]
    inside = [[2 * chip + core for chip in range(chips)] for core in range(2)]
    across = [[p * devices + 2 * chip + core for p in range(2) for chip in range(chips)] for core in range(2)]

    def exchange(rows, axes, groups):
        return lax.all_to_all(rows, axes, split_axis=0, concat_axis=0, tiled=True, axis_index_groups=groups)

    mine = [w[0] for w in (w_gate, w_up, w_down)]
    others = [lax.ppermute(w, "ep", cores) for w in mine]
    chosen = jnp.swapaxes(routes[0], 1, 2)
    gates = jnp.swapaxes(route_gates[0], 1, 2)

    at = section.astype(jnp.int32).reshape(1)
    spread = jnp.asarray(spread_matrix(tokens))
    earlier = jnp.asarray(earlier_matrix(tokens))
    order = order_matrix()
    forth, back = jnp.asarray(order), jnp.asarray(order.T)

    def near(x):
        return pltpu.with_memory_space_constraint(x, pltpu.VMEM)

    def far(x):
        return pltpu.with_memory_space_constraint(x, pltpu.HBM)

    def call(kernel, name, shapes, flops, size, limit, in_specs, scratch=()):
        return pl.pallas_call(
            kernel,
            out_shape=shapes,
            in_specs=in_specs,
            out_specs=tuple(spec() for _ in shapes) if isinstance(shapes, tuple) else spec(),
            scratch_shapes=list(scratch),
            compiler_params=pltpu.CompilerParams(vmem_limit_bytes=limit * MIB),
            cost_estimate=pl.CostEstimate(flops=flops, bytes_accessed=size, transcendentals=0),
            name=name,
        )

    scalar = spec(pltpu.SMEM)
    whole = jax.ShapeDtypeStruct((lines, part), bf16)
    halves = jax.ShapeDtypeStruct((2 * lines, part // 2), bf16)

    def run_experts(crossed, arrived):
        return call(
            functools.partial(experts_kernel, crossed),
            "experts",
            whole if crossed else halves,
            12 * received * width * half,
            12 * width * half,
            31,
            [scalar] + [spec()] * 7 + [spec(pl.ANY)] * 3,
            [
                pltpu.VMEM((PARTS, received, part), bf16),
                pltpu.VMEM((PARTS, part, 2 * half), bf16),
                pltpu.VMEM((PARTS, half, part), bf16),
                pltpu.VMEM((received, 2 * half), f32),
                pltpu.VMEM((received, 2 * half), bf16),
                pltpu.SemaphoreType.DMA((PARTS, 2)),
                pltpu.SemaphoreType.DMA((PARTS,)),
            ],
        )(at, near(arrived), norm_gain, forth, back, *[near(w) for w in mine], *others)

    packed, cross = call(
        functools.partial(first_pack, experts),
        "first_pack",
        (whole, jax.ShapeDtypeStruct((tokens + INFO, side), bf16)),
        AHEAD_FLOPS,
        4 * tokens * width * 2,
        16,
        [scalar] + [spec()] * 5,
        [pltpu.VMEM((columns, part), bf16)],
    )(at, far(own), far(chosen), far(gates), far(spread), far(earlier))
    arrived, cross = lax.optimization_barrier((exchange(packed, "ep", inside), cross))
    leaving, other = lax.optimization_barrier(
        (run_experts(False, arrived), lax.ppermute(cross, "pp", sections))
    )
    send, first_weights, last_weights = call(
        functools.partial(routing, experts, tokens),
        "routing",
        (
            jax.ShapeDtypeStruct((2, lines, columns), bf16),
            jax.ShapeDtypeStruct((2, 2 * columns, lines), bf16),
            jax.ShapeDtypeStruct((1, 2 * columns, lines), bf16),
        ),
        lines * columns * 4000,
        8 * lines * columns * 2,
        16,
        [scalar] + [spec()] * 5,
    )(at, chosen, gates, other[tokens:, :128], spread, earlier)

    returned = exchange(leaving, ("pp", "ep"), across)
    packed, kept, came = call(
        turn,
        "turn",
        (
            halves,
            pltpu.HBM((tokens, side), bf16),
            pltpu.HBM((tokens, side), bf16),
        ),
        AHEAD_FLOPS,
        8 * tokens * width * 2,
        16,
        [scalar] + [spec()] * 5,
        [pltpu.VMEM((columns, part // 2), bf16)],
    )(at, far(own), far(other), far(first_weights), near(returned), far(send))
    arrived = exchange(packed, ("pp", "ep"), across)
    kept, arrived = lax.optimization_barrier((kept, arrived))
    leaving, first_half = lax.optimization_barrier(
        (run_experts(True, arrived), lax.ppermute(kept, "pp", sections))
    )
    returned = exchange(leaving, "ep", inside)
    finished = call(
        combine,
        "combine",
        jax.ShapeDtypeStruct((tokens, width), bf16),
        4 * lines * columns * part,
        5 * tokens * width * 2,
        16,
        [spec()] * 4,
    )(first_half, came, last_weights, near(returned))
    return finished[None]


def solution(mesh):
    return jax.shard_map(
        shards,
        mesh=mesh,
        in_specs=(
            P("pp", "ep", None),
            P("pp", None),
            P("pp", None, "ep", None),
            P("pp", None, "ep", None),
            P("pp", None, "ep"),
            P("pp", None, "ep"),
            P("pp", "ep", None),
        ),
        out_specs=P("pp", "ep", None),
        check_vma=False,
    )
```

time: 595 us -> 217 us (0.36); the launches traced: 584 us -> 216 us
  waiting for transfers between devices: 203 us -> 29.3 us
  local copies, waits for them, and re-layouts: 90.8 us -> 3.9 us
  blocking collectives: 192 us -> 127 us
  Pallas kernels: 0 us -> 45.8 us
  matrix products: 44.1 us -> 0 us
  other arithmetic: 36.4 us -> 0.01 us
  starting transfers between devices: 17.9 us -> 10.1 us
    all_to_all x2 -> x1, waiting for transfers between devices: 188 us -> 29.3 us  [exchange(): lax.all_to_all(rows, axes, split_axis=0, concat_axis=0, tiled=True, axis_...]
    all_to_all x2 -> x3, blocking collectives: 192 us -> 127 us  [exchange(): lax.all_to_all(rows, axes, split_axis=0, concat_axis=0, tiled=True, axis_...]
    pallas_call x0 -> x6, Pallas kernels: none -> 45.8 us  [the longest x2 33.2 us: run_experts(): call(functools.partial(experts_kernel, crossed), 'experts', whole if cros...]
    dot_general x4 -> x0, matrix products: 44.1 us -> none  [the longest x2 30.2 us: expert_rows(): jnp.dot(hidden, w_down, preferred_element_type=jnp.float32)]
    reshape x8 -> x0, local copies, waits for them, and re-layouts: 40.4 us -> none  [the longest x2 17.1 us: expert_rows(): stacked = received.reshape(-1, width)]
    gather x6 -> x0, local copies, waits for them, and re-layouts: 35.5 us -> none  [the longest x4 29.6 us: expert_block(): outgoing = padded[sources]]
    reduce_sum x8 -> x0, other arithmetic: 32 us -> none  [the longest x2 15.7 us: expert_block(): returned.reshape(experts, SHARDS, capacity, width).astype(jnp.float32)]
    ppermute x1 -> x5, waiting for transfers between devices: 14.7 us -> 0.01 us  [the longest x3 0.01 us: shards(): others = [lax.ppermute(w, 'ep', cores) for w in mine]]
  transfers between devices with their start and end apart: 3 -> 6, of which waited for: 3 -> 1; matrix products, arithmetic and copies ran while one was open for 0% -> 0% of each run, Pallas kernels for 0% -> 18%
where the time goes in v2:
time: 217 us; the launch traced here: 216 us
  blocking collectives  127 us (59%)
  Pallas kernels  45.8 us (21%)
  waiting for transfers between devices  29.3 us (14%)
  starting transfers between devices  10.1 us (5%)
  local copies, waits for them, and re-layouts  3.9 us (2%)
    all_to_all x3, blocking collectives, exchange(): lax.all_to_all(rows, axes, split_axis=0, concat_axis=0, tiled=True, axis_...  127 us
    pallas_call x2, Pallas kernels, run_experts(): call(functools.partial(experts_kernel, crossed), 'experts', whole if cros...  33.2 us
    all_to_all x1, waiting for transfers between devices, exchange(): lax.all_to_all(rows, axes, split_axis=0, concat_axis=0, tiled=True, axis_...  29.3 us
    all_to_all x1, starting transfers between devices, exchange(): lax.all_to_all(rows, axes, split_axis=0, concat_axis=0, tiled=True, axis_...  5.38 us
    pallas_call x1, Pallas kernels, shards(): call(turn, 'turn', (halves, pltpu.HBM((tokens, side), bf16), pltpu.HBM((t...  5.25 us
  transfers between devices with their start and end apart: 6, of which 1 were waited for; matrix products, arithmetic and copies ran while one was open for 0% of the time, Pallas kernels for 18%

profile of v2, /device:TPU:0, one launch (start us, length us, event | category | flops | bytes accessed | tf_op | source)
XLA Modules:
  0.0 216.1 jit_solution(11205044893654824707)
XLA Ops:
  0.0 0.0 collective-permute-start
  0.0 0.5 collective-permute-start.1
  0.5 0.0 collective-permute-start.2
  0.5 0.0 slice-start.1
  0.5 0.0 slice-start.5
  0.5 0.0 slice-start.9
  0.6 2.7 %first_pack.1 = (bf16[768,1792]{1,0:T(8,128)(2,1)S(1)}, bf16[80,3584]{1,0:T(8,128)(2,1)S(1)}) custom-call(s32[1]{0:T(128)} %bitcast.section_ref, bf16[64,7168]{1,0:T(8,128)(2,1)} %bitcast.53, s32[2,2,64]{2,1,0:T(2,128)} %bitcast.47, f32[2,2,64]{2,1,0:T(2,128)} %bitcast.49, f32[64,256]{1,0:T(8,128)} %constant.14.clone.spread_ref, ...), custom_call_target="tpu_custom_call" | custom-call | flops 20000000000 | bytes 3670016 | tf_op jit(solution)/shard_map/first_pack/pallas_call | solution.py:376
  3.3 45.0 %all_to_all.46 = bf16[32,24,1792]{2,1,0:T(8,128)(2,1)S(1)} all-to-all(bf16[32,24,1792]{2,1,0:T(8,128)(2,1)S(1)} %bitcast.46), channel_id=1, replica_groups={{0,2,4,6,8,10,12,14,16,18,20,22,24,26,28,30,32,34,36,38,40,42,44,46,48,..., dimensions={0} | all-to-all | bytes 5505024 | tf_op jit(solution)/shard_map/all_to_all | solution.py:321
  48.3 2.9 %collective-permute-start.3 = (bf16[80,3584]{1,0:T(8,128)(2,1)S(1)}, bf16[80,3584]{1,0:T(8,128)(2,1)S(1)}, u32[]{:S(2)}, u32[]{:S(2)}) collective-permute-start(bf16[80,3584]{1,0:T(8,128)(2,1)S(1)} %get-tuple-element.24), channel_id=1, source_target_pairs={{0,64},{64,0},{1,65},{65,1},{2,66},{66,2},{3,67},{67,3},{4,68},{68... | collective-permute-start | bytes 1720328 | tf_op jit(solution)/shard_map/ppermute | solution.py:388
  51.2 0.0 collective-permute-done.g1
  51.2 0.0 collective-permute-done.1.u1
  51.2 0.0 collective-permute-done.2.d1
  51.3 15.4 %experts.2 = bf16[1536,896]{1,0:T(8,128)(2,1)} custom-call(s32[1]{0:T(128)} %bitcast.section_ref, bf16[768,1792]{1,0:T(8,128)(2,1)S(1)} %bitcast.42, f32[1,7168]{1,0:T(1,128)} %gain_ref.3, bf16[192,192]{1,0:T(8,128)(2,1)} %constant.16.clone.order_ref, bf16[192,192]{1,0:T(8,128)(2,1)} %constant.17.clone.back_ref, bf16[7168,512]{1,0:T(8,128)(2,1)S(1)} %bitcast.23, ...), custom_call_target="tpu_custom_call" | custom-call | flops 8455716864 | bytes 44040192 | tf_op jit(solution)/shard_map/experts/pallas_call | solution.py:357
  66.7 0.0 collective-permute-done.3.other_ref
  66.7 0.0 copy-start.1
  66.7 0.0 copy-start.2
  66.7 5.4 %all-to-all-start.1 = ((bf16[64,24,896]{2,1,0:T(8,128)(2,1)}), bf16[64,24,896]{2,1,0:T(8,128)(2,1)S(1)}, u32[]{:S(2)}, u32[]{:S(2)}) async-start(bf16[64,24,896]{2,1,0:T(8,128)(2,1)} %bitcast.51), calls=%async_computation.1 | async-start | bytes 5505024 | tf_op jit(solution)/shard_map/all_to_all | solution.py:321
  72.2 0.0 copy-start.3
  72.2 0.9 copy-done.3
  73.1 0.8 copy-done.4
  73.9 2.2 routing.1
  76.1 1.2 copy-done.5
  77.3 0.9 copy-done.6
  78.2 29.3 %all-to-all-done.1 = bf16[64,24,896]{2,1,0:T(8,128)(2,1)S(1)} async-done(((bf16[64,24,896]{2,1,0:T(8,128)(2,1)}), bf16[64,24,896]{2,1,0:T(8,128)(2,1)S(1)}, u32[]{:S(2)}, u32[]{:S(2)}) %all-to-all-start.1) | async-done | bytes 2752544 | tf_op jit(solution)/shard_map/all_to_all | solution.py:321
  107.5 0.0 slice-start.7
  107.5 5.3 %turn.1 = (bf16[1536,896]{1,0:T(8,128)(2,1)S(1)}, bf16[64,3584]{1,0:T(8,128)(2,1)}, bf16[64,3584]{1,0:T(8,128)(2,1)}) custom-call(s32[1]{0:T(128)} %bitcast.section_ref, bf16[64,7168]{1,0:T(8,128)(2,1)} %bitcast.54, bf16[80,3584]{1,0:T(8,128)(2,1)} %copy-done.7, bf16[2,512,768]{2,1,0:T(8,128)(2,1)} %copy-done.5, bf16[1536,896]{1,0:T(8,128)(2,1)S(1)} %bitcast.44, ...), custom_call_target="tpu_custom_call" | custom-call | flops 20000000000 | bytes 7340032 | tf_op jit(solution)/shard_map/turn/pallas_call | solution.py:405
  112.7 43.6 %all_to_all.47 = bf16[64,24,896]{2,1,0:T(8,128)(2,1)S(1)} all-to-all(bf16[64,24,896]{2,1,0:T(8,128)(2,1)S(1)} %bitcast.45), channel_id=1, replica_groups={{0,2,4,6,8,10,12,14,16,18,20,22,24,26,28,30,32,34,36,38,40,42,44,46,48,..., dimensions={0} | all-to-all | bytes 5505024 | tf_op jit(solution)/shard_map/all_to_all | solution.py:321
  156.3 1.3 collective-permute-start.4
  157.7 17.8 %experts.3 = bf16[768,1792]{1,0:T(8,128)(2,1)} custom-call(s32[1]{0:T(128)} %bitcast.section_ref, bf16[1536,896]{1,0:T(8,128)(2,1)S(1)} %bitcast.43, f32[1,7168]{1,0:T(1,128)} %gain_ref.3, bf16[192,192]{1,0:T(8,128)(2,1)} %constant.16.clone.order_ref, bf16[192,192]{1,0:T(8,128)(2,1)} %constant.17.clone.back_ref, bf16[7168,512]{1,0:T(8,128)(2,1)S(1)} %bitcast.26, ...), custom_call_target="tpu_custom_call" | custom-call | flops 8455716864 | bytes 44040192 | tf_op jit(solution)/shard_map/experts/pallas_call | solution.py:357
  175.6 0.0 collective-permute-done.4.first_ref
  175.6 38.0 %all_to_all.48 = bf16[32,24,1792]{2,1,0:T(8,128)(2,1)S(1)} all-to-all(bf16[32,24,1792]{2,1,0:T(8,128)(2,1)} %bitcast.52), channel_id=1, replica_groups={{0,2,4,6,8,10,12,14,16,18,20,22,24,26,28,30,32,34,36,38,40,42,44,46,48,..., dimensions={0} | all-to-all | bytes 5505024 | tf_op jit(solution)/shard_map/all_to_all | solution.py:321
  213.6 2.5 %combine.1 = bf16[64,7168]{1,0:T(8,128)(2,1)} custom-call(bf16[64,3584]{1,0:T(8,128)(2,1)S(1)} %collective-permute-done.4.first_ref, bf16[64,3584]{1,0:T(8,128)(2,1)S(1)} %copy-done, bf16[1,512,768]{2,1,0:T(8,128)(2,1)S(1)} %get-tuple-element.35.weights_ref, bf16[768,1792]{1,0:T(8,128)(2,1)S(1)} %bitcast.41), custom_call_target="tpu_custom_call" | custom-call | flops 1409286144 | bytes 4587520 | tf_op jit(solution)/shard_map/combine/pallas_call | solution.py:425
  (38 shorter events, 0.1 us)
Async XLA Ops:
  0.0 51.2 %collective-permute-start = (bf16[7168,512]{1,0:T(8,128)(2,1)}, bf16[7168,512]{1,0:T(8,128)(2,1)}, u32[]{:S(2)}, u32[]{:S(2)}) collective-permute-start(bf16[7168,512]{1,0:T(8,128)(2,1)} %bitcast.20), channel_id=1, source_target_pairs={{0,1},{1,0},{2,3},{3,2},{4,5},{5,4},{6,7},{7,6},{8,9},{9,8},{10,11... | collective-permute-start | bytes 22020104 | tf_op jit(solution)/shard_map/ppermute | solution.py:324
  0.0 51.2 %collective-permute-start.1 = (bf16[7168,512]{1,0:T(8,128)(2,1)}, bf16[7168,512]{1,0:T(8,128)(2,1)}, u32[]{:S(2)}, u32[]{:S(2)}) collective-permute-start(bf16[7168,512]{1,0:T(8,128)(2,1)} %bitcast.27), channel_id=1, source_target_pairs={{0,1},{1,0},{2,3},{3,2},{4,5},{5,4},{6,7},{7,6},{8,9},{9,8},{10,11... | collective-permute-start | bytes 22020104 | tf_op jit(solution)/shard_map/ppermute | solution.py:324
  0.5 50.7 %collective-permute-start.2 = (bf16[512,7168]{1,0:T(8,128)(2,1)}, bf16[512,7168]{1,0:T(8,128)(2,1)}, u32[]{:S(2)}, u32[]{:S(2)}) collective-permute-start(bf16[512,7168]{1,0:T(8,128)(2,1)} %bitcast.34), channel_id=1, source_target_pairs={{0,1},{1,0},{2,3},{3,2},{4,5},{5,4},{6,7},{7,6},{8,9},{9,8},{10,11... | collective-permute-start | bytes 22020104 | tf_op jit(solution)/shard_map/ppermute | solution.py:324
  0.5 50.7 %slice-start = ((s8[7340032]{0:T(1024)(128)(4,1)}), s8[4194304]{0:T(1024)(128)(4,1)S(1)}, s32[]{:S(2)}) async-start(s8[7340032]{0:T(1024)(128)(4,1)} %bitcast.21), calls=%async_computation.4 | async-start | bytes 8388608
  0.5 50.7 %slice-start.4 = ((s8[7340032]{0:T(1024)(128)(4,1)}), s8[4194304]{0:T(1024)(128)(4,1)S(1)}, s32[]{:S(2)}) async-start(s8[7340032]{0:T(1024)(128)(4,1)} %bitcast.28), calls=%async_computation.8 | async-start | bytes 8388608
  0.5 50.7 %slice-start.8 = ((s8[7340032]{0:T(1024)(128)(4,1)}), s8[4194304]{0:T(1024)(128)(4,1)S(1)}, s32[]{:S(2)}) async-start(s8[7340032]{0:T(1024)(128)(4,1)} %bitcast.35), calls=%async_computation.12 | async-start | bytes 8388608
  0.5 50.7 %slice-start.1 = ((s8[7340032]{0:T(1024)(128)(4,1)}), s8[3145728]{0:T(1024)(128)(4,1)S(1)}, s32[]{:S(2)}) async-start(s8[7340032]{0:T(1024)(128)(4,1)} %bitcast.21), calls=%async_computation.5 | async-start | bytes 6291456
  0.5 50.7 %slice-start.5 = ((s8[7340032]{0:T(1024)(128)(4,1)}), s8[3145728]{0:T(1024)(128)(4,1)S(1)}, s32[]{:S(2)}) async-start(s8[7340032]{0:T(1024)(128)(4,1)} %bitcast.28), calls=%async_computation.9 | async-start | bytes 6291456
  0.5 50.7 %slice-start.9 = ((s8[7340032]{0:T(1024)(128)(4,1)}), s8[3145728]{0:T(1024)(128)(4,1)S(1)}, s32[]{:S(2)}) async-start(s8[7340032]{0:T(1024)(128)(4,1)} %bitcast.35), calls=%async_computation.13 | async-start | bytes 6291456
  48.3 18.4 %collective-permute-start.3 = (bf16[80,3584]{1,0:T(8,128)(2,1)S(1)}, bf16[80,3584]{1,0:T(8,128)(2,1)S(1)}, u32[]{:S(2)}, u32[]{:S(2)}) collective-permute-start(bf16[80,3584]{1,0:T(8,128)(2,1)S(1)} %get-tuple-element.24), channel_id=1, source_target_pairs={{0,64},{64,0},{1,65},{65,1},{2,66},{66,2},{3,67},{67,3},{4,68},{68... | collective-permute-start | bytes 1720328 | tf_op jit(solution)/shard_map/ppermute | solution.py:388
  66.7 5.4 %copy-start.7 = (bf16[80,3584]{1,0:T(8,128)(2,1)}, bf16[80,3584]{1,0:T(8,128)(2,1)S(1)}, u32[]{:S(2)}) copy-start(bf16[80,3584]{1,0:T(8,128)(2,1)S(1)} %collective-permute-done.3.other_ref) | copy-start | bytes 1720324
  66.7 5.4 %copy-start.1 = (s32[1,2,64,2]{2,3,1,0:T(2,128)S(1)}, s32[1,2,64,2]{2,3,1,0:T(2,128)}, u32[]{:S(2)}) copy-start(s32[1,2,64,2]{2,3,1,0:T(2,128)} %param.13) | copy-start | bytes 3076
  66.7 5.4 %copy-start.2 = (f32[1,2,64,2]{2,3,1,0:T(2,128)S(1)}, f32[1,2,64,2]{2,3,1,0:T(2,128)}, u32[]{:S(2)}) copy-start(f32[1,2,64,2]{2,3,1,0:T(2,128)} %param.14) | copy-start | bytes 3076
  66.7 40.7 %all-to-all-start.1 = ((bf16[64,24,896]{2,1,0:T(8,128)(2,1)}), bf16[64,24,896]{2,1,0:T(8,128)(2,1)S(1)}, u32[]{:S(2)}, u32[]{:S(2)}) async-start(bf16[64,24,896]{2,1,0:T(8,128)(2,1)} %bitcast.51), calls=%async_computation.1 | async-start | bytes 5505024 | tf_op jit(solution)/shard_map/all_to_all | solution.py:321
  72.2 0.9 copy-start.3
  73.1 0.8 copy-start.4
  76.1 1.2 copy-start.5
  77.3 0.9 copy-start.6
  107.5 50.2 %slice-start.2 = ((s8[7340032]{0:T(1024)(128)(4,1)}), s8[4194304]{0:T(1024)(128)(4,1)S(1)}, s32[]{:S(2)}) async-start(s8[7340032]{0:T(1024)(128)(4,1)} %bitcast.24), calls=%async_computation.6 | async-start | bytes 8388608
  107.5 50.2 %slice-start.6 = ((s8[7340032]{0:T(1024)(128)(4,1)}), s8[4194304]{0:T(1024)(128)(4,1)S(1)}, s32[]{:S(2)}) async-start(s8[7340032]{0:T(1024)(128)(4,1)} %bitcast.31), calls=%async_computation.10 | async-start | bytes 8388608
  107.5 50.2 %slice-start.10 = ((s8[7340032]{0:T(1024)(128)(4,1)}), s8[4194304]{0:T(1024)(128)(4,1)S(1)}, s32[]{:S(2)}) async-start(s8[7340032]{0:T(1024)(128)(4,1)} %bitcast.38), calls=%async_computation.14 | async-start | bytes 8388608
  107.5 50.2 %slice-start.3 = ((s8[7340032]{0:T(1024)(128)(4,1)}), s8[3145728]{0:T(1024)(128)(4,1)S(1)}, s32[]{:S(2)}) async-start(s8[7340032]{0:T(1024)(128)(4,1)} %bitcast.24), calls=%async_computation.7 | async-start | bytes 6291456
  107.5 50.2 %slice-start.7 = ((s8[7340032]{0:T(1024)(128)(4,1)}), s8[3145728]{0:T(1024)(128)(4,1)S(1)}, s32[]{:S(2)}) async-start(s8[7340032]{0:T(1024)(128)(4,1)} %bitcast.31), calls=%async_computation.11 | async-start | bytes 6291456
  107.5 50.2 %slice-start.11 = ((s8[7340032]{0:T(1024)(128)(4,1)}), s8[3145728]{0:T(1024)(128)(4,1)S(1)}, s32[]{:S(2)}) async-start(s8[7340032]{0:T(1024)(128)(4,1)} %bitcast.38), calls=%async_computation.15 | async-start | bytes 6291456
  112.7 43.6 %copy-start.8 = (bf16[64,3584]{1,0:T(8,128)(2,1)S(1)}, bf16[64,3584]{1,0:T(8,128)(2,1)}, u32[]{:S(2)}) copy-start(bf16[64,3584]{1,0:T(8,128)(2,1)} %get-tuple-element.32) | copy-start | bytes 1376260
  156.3 19.2 %collective-permute-start.4 = (bf16[64,3584]{1,0:T(8,128)(2,1)S(1)}, bf16[64,3584]{1,0:T(8,128)(2,1)S(1)}, u32[]{:S(2)}, u32[]{:S(2)}) collective-permute-start(bf16[64,3584]{1,0:T(8,128)(2,1)S(1)} %copy-done.8), channel_id=1, source_target_pairs={{0,64},{64,0},{1,65},{65,1},{2,66},{66,2},{3,67},{67,3},{4,68},{68... | collective-permute-start | bytes 1376264 | tf_op jit(solution)/shard_map/ppermute | solution.py:422
  175.6 38.0 %copy-start = (bf16[64,3584]{1,0:T(8,128)(2,1)S(1)}, bf16[64,3584]{1,0:T(8,128)(2,1)}, u32[]{:S(2)}) copy-start(bf16[64,3584]{1,0:T(8,128)(2,1)} %get-tuple-element.34.second_ref) | copy-start | bytes 1376260

commit v3 on v2

--- a/solution.py
+++ b/solution.py
@@ -32,6 +32,15 @@
     return jnp.where(condition, 1.0, 0.0).astype(bf16)
 
 
+def chip_order():
+    return [x * 8 + y * 4 + z for y in range(2) for x in range(4) for z in range(4)]
+
+
+def place_on_path(chip):
+    x, y, z = chip >> 3, jnp.bitwise_and(chip >> 2, 1), jnp.bitwise_and(chip, 3)
+    return y * 16 + x * 4 + z
+
+
 def earlier_matrix(tokens):
     size = PARTS * tokens
     a, b = np.arange(size)[:, None], np.arange(size)[None, :]
@@ -55,7 +64,7 @@
 def selection(routes, spread_ref, earlier_ref, tokens, experts):
     rows, columns = experts * ROWS, PARTS * tokens
     chosen = jnp.dot(routes, spread_ref[...], preferred_element_type=f32, precision=lax.Precision.HIGHEST)
-    chosen = chosen.astype(jnp.int32)
+    chosen = place_on_path(chosen.astype(jnp.int32))
     row = lax.broadcasted_iota(jnp.int32, (rows, 128), 0)
     expert = (row * 2731) >> 16
     rest = row - expert * ROWS
@@ -314,8 +323,8 @@
 
     sections = [(0, 1), (1, 0)]
     cores = [(device, device ^ 1) for device in range(devices)]
-    inside = [[2 * chip + core for chip in range(chips)] for core in range(2)]
-    across = [[p * devices + 2 * chip + core for p in range(2) for chip in range(chips)] for core in range(2)]
+    inside = [[2 * chip + core for chip in chip_order()] for core in range(2)]
+    across = [[p * devices + 2 * chip + core for p in range(2) for chip in chip_order()] for core in range(2)]
 
     def exchange(rows, axes, groups):
         return lax.all_to_all(rows, axes, split_axis=0, concat_axis=0, tiled=True, axis_index_groups=groups)

time: 217 us -> 214 us (0.986)
  blocking collectives: 127 us -> 124 us
    all_to_all x3, blocking collectives: 127 us -> 124 us  [exchange(): lax.all_to_all(rows, axes, split_axis=0, concat_axis=0, tiled=True, axis_...]
where the time goes in v3:
time: 214 us
  blocking collectives  124 us (58%)
  Pallas kernels  45.9 us (21%)
  waiting for transfers between devices  29.5 us (14%)
  starting transfers between devices  10.4 us (5%)
  local copies, waits for them, and re-layouts  3.9 us (2%)
    all_to_all x3, blocking collectives, exchange(): lax.all_to_all(rows, axes, split_axis=0, concat_axis=0, tiled=True, axis_...  124 us
    pallas_call x2, Pallas kernels, run_experts(): call(functools.partial(experts_kernel, crossed), 'experts', whole if cros...  33.2 us
    all_to_all x1, waiting for transfers between devices, exchange(): lax.all_to_all(rows, axes, split_axis=0, concat_axis=0, tiled=True, axis_...  29.5 us
    all_to_all x1, starting transfers between devices, exchange(): lax.all_to_all(rows, axes, split_axis=0, concat_axis=0, tiled=True, axis_...  6.34 us
    pallas_call x1, Pallas kernels, shards(): call(turn, 'turn', (halves, pltpu.HBM((tokens, side), bf16), pltpu.HBM((t...  5.25 us
  transfers between devices with their start and end apart: 6, of which 1 were waited for; matrix products, arithmetic and copies ran while one was open for 0% of the time, Pallas kernels for 18%

profile of v3, /device:TPU:0, one launch (start us, length us, event | category | flops | bytes accessed | tf_op | source)
XLA Modules:
  0.0 213.7 jit_solution(15673588059372174275)
XLA Ops:
  0.0 0.0 collective-permute-start
  0.0 0.5 collective-permute-start.1
  0.5 0.0 collective-permute-start.2
  0.5 0.0 slice-start.1
  0.5 0.0 slice-start.5
  0.5 0.0 slice-start.9
  0.6 2.7 %first_pack.1 = (bf16[768,1792]{1,0:T(8,128)(2,1)S(1)}, bf16[80,3584]{1,0:T(8,128)(2,1)S(1)}) custom-call(s32[1]{0:T(128)} %bitcast.section_ref, bf16[64,7168]{1,0:T(8,128)(2,1)} %bitcast.53, s32[2,2,64]{2,1,0:T(2,128)} %bitcast.47, f32[2,2,64]{2,1,0:T(2,128)} %bitcast.49, f32[64,256]{1,0:T(8,128)} %constant.14.clone.spread_ref, ...), custom_call_target="tpu_custom_call" | custom-call | flops 20000000000 | bytes 3670016 | tf_op jit(solution)/shard_map/first_pack/pallas_call | solution.py:385
  3.3 45.1 %all_to_all.46 = bf16[32,24,1792]{2,1,0:T(8,128)(2,1)S(1)} all-to-all(bf16[32,24,1792]{2,1,0:T(8,128)(2,1)S(1)} %bitcast.46), channel_id=1, replica_groups={{0,2,4,6,16,18,20,22,32,34,36,38,48,50,52,54,8,10,12,14,24,26,28,30,40,..., dimensions={0} | all-to-all | bytes 5505024 | tf_op jit(solution)/shard_map/all_to_all | solution.py:330
  48.4 2.9 %collective-permute-start.3 = (bf16[80,3584]{1,0:T(8,128)(2,1)S(1)}, bf16[80,3584]{1,0:T(8,128)(2,1)S(1)}, u32[]{:S(2)}, u32[]{:S(2)}) collective-permute-start(bf16[80,3584]{1,0:T(8,128)(2,1)S(1)} %get-tuple-element.24), channel_id=1, source_target_pairs={{0,64},{64,0},{1,65},{65,1},{2,66},{66,2},{3,67},{67,3},{4,68},{68... | collective-permute-start | bytes 1720328 | tf_op jit(solution)/shard_map/ppermute | solution.py:397
  51.3 0.0 collective-permute-done.g1
  51.3 0.0 collective-permute-done.1.u1
  51.3 0.0 collective-permute-done.2.d1
  51.4 15.4 %experts.2 = bf16[1536,896]{1,0:T(8,128)(2,1)} custom-call(s32[1]{0:T(128)} %bitcast.section_ref, bf16[768,1792]{1,0:T(8,128)(2,1)S(1)} %bitcast.42, f32[1,7168]{1,0:T(1,128)} %gain_ref.3, bf16[192,192]{1,0:T(8,128)(2,1)} %constant.16.clone.order_ref, bf16[192,192]{1,0:T(8,128)(2,1)} %constant.17.clone.back_ref, bf16[7168,512]{1,0:T(8,128)(2,1)S(1)} %bitcast.23, ...), custom_call_target="tpu_custom_call" | custom-call | flops 8455716864 | bytes 44040192 | tf_op jit(solution)/shard_map/experts/pallas_call | solution.py:366
  66.8 0.0 collective-permute-done.3.other_ref
  66.8 0.0 copy-start.1
  66.8 0.0 copy-start.2
  66.8 6.3 %all-to-all-start.1 = ((bf16[64,24,896]{2,1,0:T(8,128)(2,1)}), bf16[64,24,896]{2,1,0:T(8,128)(2,1)S(1)}, u32[]{:S(2)}, u32[]{:S(2)}) async-start(bf16[64,24,896]{2,1,0:T(8,128)(2,1)} %bitcast.51), calls=%async_computation.1 | async-start | bytes 5505024 | tf_op jit(solution)/shard_map/all_to_all | solution.py:330
  73.2 0.0 copy-start.3
  73.2 0.9 copy-done.3
  74.1 0.8 copy-done.4
  75.0 2.2 %routing.1 = (bf16[2,768,256]{2,1,0:T(8,128)(2,1)S(1)}, bf16[2,512,768]{2,1,0:T(8,128)(2,1)S(1)}, bf16[1,512,768]{2,1,0:T(8,128)(2,1)S(1)}) custom-call(s32[1]{0:T(128)} %bitcast.section_ref, s32[2,2,64]{2,1,0:T(2,128)S(1)} %bitcast.48, f32[2,2,64]{2,1,0:T(2,128)S(1)} %bitcast.50, bf16[16,128]{1,0:T(8,128)(2,1)S(1)} %slice.3.cross_ref, ...), custom_call_target="tpu_custom_call" | custom-call | flops 786432000 | bytes 3145728 | tf_op jit(solution)/shard_map/routing/pallas_call | solution.py:399
  77.2 1.2 copy-done.5
  78.4 0.9 copy-done.6
  79.3 29.5 %all-to-all-done.1 = bf16[64,24,896]{2,1,0:T(8,128)(2,1)S(1)} async-done(((bf16[64,24,896]{2,1,0:T(8,128)(2,1)}), bf16[64,24,896]{2,1,0:T(8,128)(2,1)S(1)}, u32[]{:S(2)}, u32[]{:S(2)}) %all-to-all-start.1) | async-done | bytes 2752544 | tf_op jit(solution)/shard_map/all_to_all | solution.py:330
  108.8 0.0 slice-start.7
  108.8 5.3 %turn.1 = (bf16[1536,896]{1,0:T(8,128)(2,1)S(1)}, bf16[64,3584]{1,0:T(8,128)(2,1)}, bf16[64,3584]{1,0:T(8,128)(2,1)}) custom-call(s32[1]{0:T(128)} %bitcast.section_ref, bf16[64,7168]{1,0:T(8,128)(2,1)} %bitcast.54, bf16[80,3584]{1,0:T(8,128)(2,1)} %copy-done.7, bf16[2,512,768]{2,1,0:T(8,128)(2,1)} %copy-done.5, bf16[1536,896]{1,0:T(8,128)(2,1)S(1)} %bitcast.44, ...), custom_call_target="tpu_custom_call" | custom-call | flops 20000000000 | bytes 7340032 | tf_op jit(solution)/shard_map/turn/pallas_call | solution.py:414
  114.1 41.8 %all_to_all.47 = bf16[64,24,896]{2,1,0:T(8,128)(2,1)S(1)} all-to-all(bf16[64,24,896]{2,1,0:T(8,128)(2,1)S(1)} %bitcast.45), channel_id=1, replica_groups={{0,2,4,6,16,18,20,22,32,34,36,38,48,50,52,54,8,10,12,14,24,26,28,30,40,..., dimensions={0} | all-to-all | bytes 5505024 | tf_op jit(solution)/shard_map/all_to_all | solution.py:330
  155.9 0.7 collective-permute-start.4
  156.7 17.8 %experts.3 = bf16[768,1792]{1,0:T(8,128)(2,1)} custom-call(s32[1]{0:T(128)} %bitcast.section_ref, bf16[1536,896]{1,0:T(8,128)(2,1)S(1)} %bitcast.43, f32[1,7168]{1,0:T(1,128)} %gain_ref.3, bf16[192,192]{1,0:T(8,128)(2,1)} %constant.16.clone.order_ref, bf16[192,192]{1,0:T(8,128)(2,1)} %constant.17.clone.back_ref, bf16[7168,512]{1,0:T(8,128)(2,1)S(1)} %bitcast.26, ...), custom_call_target="tpu_custom_call" | custom-call | flops 8455716864 | bytes 44040192 | tf_op jit(solution)/shard_map/experts/pallas_call | solution.py:366
  174.5 0.0 collective-permute-done.4.first_ref
  174.5 36.7 %all_to_all.48 = bf16[32,24,1792]{2,1,0:T(8,128)(2,1)S(1)} all-to-all(bf16[32,24,1792]{2,1,0:T(8,128)(2,1)} %bitcast.52), channel_id=1, replica_groups={{0,2,4,6,16,18,20,22,32,34,36,38,48,50,52,54,8,10,12,14,24,26,28,30,40,..., dimensions={0} | all-to-all | bytes 5505024 | tf_op jit(solution)/shard_map/all_to_all | solution.py:330
  211.2 2.5 %combine.1 = bf16[64,7168]{1,0:T(8,128)(2,1)} custom-call(bf16[64,3584]{1,0:T(8,128)(2,1)S(1)} %collective-permute-done.4.first_ref, bf16[64,3584]{1,0:T(8,128)(2,1)S(1)} %copy-done, bf16[1,512,768]{2,1,0:T(8,128)(2,1)S(1)} %get-tuple-element.35.weights_ref, bf16[768,1792]{1,0:T(8,128)(2,1)S(1)} %bitcast.41), custom_call_target="tpu_custom_call" | custom-call | flops 1409286144 | bytes 4587520 | tf_op jit(solution)/shard_map/combine/pallas_call | solution.py:434
  (38 shorter events, 0.1 us)
Async XLA Ops:
  0.0 51.3 %collective-permute-start = (bf16[7168,512]{1,0:T(8,128)(2,1)}, bf16[7168,512]{1,0:T(8,128)(2,1)}, u32[]{:S(2)}, u32[]{:S(2)}) collective-permute-start(bf16[7168,512]{1,0:T(8,128)(2,1)} %bitcast.20), channel_id=1, source_target_pairs={{0,1},{1,0},{2,3},{3,2},{4,5},{5,4},{6,7},{7,6},{8,9},{9,8},{10,11... | collective-permute-start | bytes 22020104 | tf_op jit(solution)/shard_map/ppermute | solution.py:333
  0.0 51.3 %collective-permute-start.1 = (bf16[7168,512]{1,0:T(8,128)(2,1)}, bf16[7168,512]{1,0:T(8,128)(2,1)}, u32[]{:S(2)}, u32[]{:S(2)}) collective-permute-start(bf16[7168,512]{1,0:T(8,128)(2,1)} %bitcast.27), channel_id=1, source_target_pairs={{0,1},{1,0},{2,3},{3,2},{4,5},{5,4},{6,7},{7,6},{8,9},{9,8},{10,11... | collective-permute-start | bytes 22020104 | tf_op jit(solution)/shard_map/ppermute | solution.py:333
  0.5 50.8 %collective-permute-start.2 = (bf16[512,7168]{1,0:T(8,128)(2,1)}, bf16[512,7168]{1,0:T(8,128)(2,1)}, u32[]{:S(2)}, u32[]{:S(2)}) collective-permute-start(bf16[512,7168]{1,0:T(8,128)(2,1)} %bitcast.34), channel_id=1, source_target_pairs={{0,1},{1,0},{2,3},{3,2},{4,5},{5,4},{6,7},{7,6},{8,9},{9,8},{10,11... | collective-permute-start | bytes 22020104 | tf_op jit(solution)/shard_map/ppermute | solution.py:333
  0.5 50.8 %slice-start = ((s8[7340032]{0:T(1024)(128)(4,1)}), s8[4194304]{0:T(1024)(128)(4,1)S(1)}, s32[]{:S(2)}) async-start(s8[7340032]{0:T(1024)(128)(4,1)} %bitcast.21), calls=%async_computation.4 | async-start | bytes 8388608
  0.5 50.8 %slice-start.4 = ((s8[7340032]{0:T(1024)(128)(4,1)}), s8[4194304]{0:T(1024)(128)(4,1)S(1)}, s32[]{:S(2)}) async-start(s8[7340032]{0:T(1024)(128)(4,1)} %bitcast.28), calls=%async_computation.8 | async-start | bytes 8388608
  0.5 50.8 %slice-start.8 = ((s8[7340032]{0:T(1024)(128)(4,1)}), s8[4194304]{0:T(1024)(128)(4,1)S(1)}, s32[]{:S(2)}) async-start(s8[7340032]{0:T(1024)(128)(4,1)} %bitcast.35), calls=%async_computation.12 | async-start | bytes 8388608
  0.5 50.8 %slice-start.1 = ((s8[7340032]{0:T(1024)(128)(4,1)}), s8[3145728]{0:T(1024)(128)(4,1)S(1)}, s32[]{:S(2)}) async-start(s8[7340032]{0:T(1024)(128)(4,1)} %bitcast.21), calls=%async_computation.5 | async-start | bytes 6291456
  0.5 50.8 %slice-start.5 = ((s8[7340032]{0:T(1024)(128)(4,1)}), s8[3145728]{0:T(1024)(128)(4,1)S(1)}, s32[]{:S(2)}) async-start(s8[7340032]{0:T(1024)(128)(4,1)} %bitcast.28), calls=%async_computation.9 | async-start | bytes 6291456
  0.5 50.8 %slice-start.9 = ((s8[7340032]{0:T(1024)(128)(4,1)}), s8[3145728]{0:T(1024)(128)(4,1)S(1)}, s32[]{:S(2)}) async-start(s8[7340032]{0:T(1024)(128)(4,1)} %bitcast.35), calls=%async_computation.13 | async-start | bytes 6291456
  48.4 18.4 %collective-permute-start.3 = (bf16[80,3584]{1,0:T(8,128)(2,1)S(1)}, bf16[80,3584]{1,0:T(8,128)(2,1)S(1)}, u32[]{:S(2)}, u32[]{:S(2)}) collective-permute-start(bf16[80,3584]{1,0:T(8,128)(2,1)S(1)} %get-tuple-element.24), channel_id=1, source_target_pairs={{0,64},{64,0},{1,65},{65,1},{2,66},{66,2},{3,67},{67,3},{4,68},{68... | collective-permute-start | bytes 1720328 | tf_op jit(solution)/shard_map/ppermute | solution.py:397
  66.8 6.4 %copy-start.7 = (bf16[80,3584]{1,0:T(8,128)(2,1)}, bf16[80,3584]{1,0:T(8,128)(2,1)S(1)}, u32[]{:S(2)}) copy-start(bf16[80,3584]{1,0:T(8,128)(2,1)S(1)} %collective-permute-done.3.other_ref) | copy-start | bytes 1720324
  66.8 6.4 %copy-start.1 = (s32[1,2,64,2]{2,3,1,0:T(2,128)S(1)}, s32[1,2,64,2]{2,3,1,0:T(2,128)}, u32[]{:S(2)}) copy-start(s32[1,2,64,2]{2,3,1,0:T(2,128)} %param.13) | copy-start | bytes 3076
  66.8 6.4 %copy-start.2 = (f32[1,2,64,2]{2,3,1,0:T(2,128)S(1)}, f32[1,2,64,2]{2,3,1,0:T(2,128)}, u32[]{:S(2)}) copy-start(f32[1,2,64,2]{2,3,1,0:T(2,128)} %param.14) | copy-start | bytes 3076
  66.8 41.9 %all-to-all-start.1 = ((bf16[64,24,896]{2,1,0:T(8,128)(2,1)}), bf16[64,24,896]{2,1,0:T(8,128)(2,1)S(1)}, u32[]{:S(2)}, u32[]{:S(2)}) async-start(bf16[64,24,896]{2,1,0:T(8,128)(2,1)} %bitcast.51), calls=%async_computation.1 | async-start | bytes 5505024 | tf_op jit(solution)/shard_map/all_to_all | solution.py:330
  73.2 0.9 copy-start.3
  74.1 0.8 copy-start.4
  77.2 1.2 copy-start.5
  78.4 0.9 copy-start.6
  108.8 47.8 %slice-start.2 = ((s8[7340032]{0:T(1024)(128)(4,1)}), s8[4194304]{0:T(1024)(128)(4,1)S(1)}, s32[]{:S(2)}) async-start(s8[7340032]{0:T(1024)(128)(4,1)} %bitcast.24), calls=%async_computation.6 | async-start | bytes 8388608
  108.8 47.8 %slice-start.6 = ((s8[7340032]{0:T(1024)(128)(4,1)}), s8[4194304]{0:T(1024)(128)(4,1)S(1)}, s32[]{:S(2)}) async-start(s8[7340032]{0:T(1024)(128)(4,1)} %bitcast.31), calls=%async_computation.10 | async-start | bytes 8388608
  108.8 47.8 %slice-start.10 = ((s8[7340032]{0:T(1024)(128)(4,1)}), s8[4194304]{0:T(1024)(128)(4,1)S(1)}, s32[]{:S(2)}) async-start(s8[7340032]{0:T(1024)(128)(4,1)} %bitcast.38), calls=%async_computation.14 | async-start | bytes 8388608
  108.8 47.8 %slice-start.3 = ((s8[7340032]{0:T(1024)(128)(4,1)}), s8[3145728]{0:T(1024)(128)(4,1)S(1)}, s32[]{:S(2)}) async-start(s8[7340032]{0:T(1024)(128)(4,1)} %bitcast.24), calls=%async_computation.7 | async-start | bytes 6291456
  108.8 47.8 %slice-start.7 = ((s8[7340032]{0:T(1024)(128)(4,1)}), s8[3145728]{0:T(1024)(128)(4,1)S(1)}, s32[]{:S(2)}) async-start(s8[7340032]{0:T(1024)(128)(4,1)} %bitcast.31), calls=%async_computation.11 | async-start | bytes 6291456
  108.8 47.8 %slice-start.11 = ((s8[7340032]{0:T(1024)(128)(4,1)}), s8[3145728]{0:T(1024)(128)(4,1)S(1)}, s32[]{:S(2)}) async-start(s8[7340032]{0:T(1024)(128)(4,1)} %bitcast.38), calls=%async_computation.15 | async-start | bytes 6291456
  114.1 41.8 %copy-start.8 = (bf16[64,3584]{1,0:T(8,128)(2,1)S(1)}, bf16[64,3584]{1,0:T(8,128)(2,1)}, u32[]{:S(2)}) copy-start(bf16[64,3584]{1,0:T(8,128)(2,1)} %get-tuple-element.32) | copy-start | bytes 1376260
  155.9 18.6 %collective-permute-start.4 = (bf16[64,3584]{1,0:T(8,128)(2,1)S(1)}, bf16[64,3584]{1,0:T(8,128)(2,1)S(1)}, u32[]{:S(2)}, u32[]{:S(2)}) collective-permute-start(bf16[64,3584]{1,0:T(8,128)(2,1)S(1)} %copy-done.8), channel_id=1, source_target_pairs={{0,64},{64,0},{1,65},{65,1},{2,66},{66,2},{3,67},{67,3},{4,68},{68... | collective-permute-start | bytes 1376264 | tf_op jit(solution)/shard_map/ppermute | solution.py:431
  174.5 36.7 %copy-start = (bf16[64,3584]{1,0:T(8,128)(2,1)S(1)}, bf16[64,3584]{1,0:T(8,128)(2,1)}, u32[]{:S(2)}) copy-start(bf16[64,3584]{1,0:T(8,128)(2,1)} %get-tuple-element.34.second_ref) | copy-start | bytes 1376260

commit v4 on v3

--- a/solution.py
+++ b/solution.py
@@ -15,7 +15,7 @@
 GROUP = 8
 TAKE = GROUP * SLOTS
 SIZE = GROUP * ROWS
-AHEAD = 1
+AHEAD = 0
 AHEAD_FLOPS = 20_000_000_000
 INFO = 16
 MIB = 1024 * 1024

time: 214 us -> 217 us (1.014)
  Pallas kernels: 45.9 us -> 48.6 us
    pallas_call x2, Pallas kernels: 33.2 us -> 35.9 us  [run_experts(): call(functools.partial(experts_kernel, crossed), 'experts', whole if cros...]
  transfers between devices with their start and end apart: 6 -> 6, of which waited for: 1 -> 1; matrix products, arithmetic and copies ran while one was open for 0% -> 0% of each run, Pallas kernels for 18% -> 19%
where the time goes in v4:
time: 217 us; the launch traced here: 216 us
  blocking collectives  124 us (57%)
  Pallas kernels  48.6 us (22%)
  waiting for transfers between devices  29.6 us (14%)
  starting transfers between devices  10.4 us (5%)
  local copies, waits for them, and re-layouts  3.9 us (2%)
    all_to_all x3, blocking collectives, exchange(): lax.all_to_all(rows, axes, split_axis=0, concat_axis=0, tiled=True, axis_...  124 us
    pallas_call x2, Pallas kernels, run_experts(): call(functools.partial(experts_kernel, crossed), 'experts', whole if cros...  35.9 us
    all_to_all x1, waiting for transfers between devices, exchange(): lax.all_to_all(rows, axes, split_axis=0, concat_axis=0, tiled=True, axis_...  29.5 us
    all_to_all x1, starting transfers between devices, exchange(): lax.all_to_all(rows, axes, split_axis=0, concat_axis=0, tiled=True, axis_...  6.33 us
    pallas_call x1, Pallas kernels, shards(): call(turn, 'turn', (halves, pltpu.HBM((tokens, side), bf16), pltpu.HBM((t...  5.25 us
  transfers between devices with their start and end apart: 6, of which 1 were waited for; matrix products, arithmetic and copies ran while one was open for 0% of the time, Pallas kernels for 19%

profile of v4, /device:TPU:0, one launch (start us, length us, event | category | flops | bytes accessed | tf_op | source)
XLA Modules:
  0.0 216.5 jit_solution(9984033041764511973)
XLA Ops:
  0.0 0.0 collective-permute-start
  0.0 0.5 collective-permute-start.1
  0.5 0.0 collective-permute-start.2
  0.5 0.0 slice-start.1
  0.5 0.0 slice-start.5
  0.5 0.0 slice-start.9
  0.6 2.7 %first_pack.1 = (bf16[768,1792]{1,0:T(8,128)(2,1)S(1)}, bf16[80,3584]{1,0:T(8,128)(2,1)S(1)}) custom-call(s32[1]{0:T(128)} %bitcast.section_ref, bf16[64,7168]{1,0:T(8,128)(2,1)} %bitcast.53, s32[2,2,64]{2,1,0:T(2,128)} %bitcast.47, f32[2,2,64]{2,1,0:T(2,128)} %bitcast.49, f32[64,256]{1,0:T(8,128)} %constant.14.clone.spread_ref, ...), custom_call_target="tpu_custom_call" | custom-call | flops 20000000000 | bytes 3670016 | tf_op jit(solution)/shard_map/first_pack/pallas_call | solution.py:385
  3.3 45.1 %all_to_all.46 = bf16[32,24,1792]{2,1,0:T(8,128)(2,1)S(1)} all-to-all(bf16[32,24,1792]{2,1,0:T(8,128)(2,1)S(1)} %bitcast.46), channel_id=1, replica_groups={{0,2,4,6,16,18,20,22,32,34,36,38,48,50,52,54,8,10,12,14,24,26,28,30,40,..., dimensions={0} | all-to-all | bytes 5505024 | tf_op jit(solution)/shard_map/all_to_all | solution.py:330
  48.4 2.9 %collective-permute-start.3 = (bf16[80,3584]{1,0:T(8,128)(2,1)S(1)}, bf16[80,3584]{1,0:T(8,128)(2,1)S(1)}, u32[]{:S(2)}, u32[]{:S(2)}) collective-permute-start(bf16[80,3584]{1,0:T(8,128)(2,1)S(1)} %get-tuple-element.24), channel_id=1, source_target_pairs={{0,64},{64,0},{1,65},{65,1},{2,66},{66,2},{3,67},{67,3},{4,68},{68... | collective-permute-start | bytes 1720328 | tf_op jit(solution)/shard_map/ppermute | solution.py:397
  51.3 0.0 collective-permute-done.g1
  51.3 0.0 collective-permute-done.1.u1
  51.3 0.0 collective-permute-done.2.d1
  51.4 18.1 %experts.2 = bf16[1536,896]{1,0:T(8,128)(2,1)} custom-call(s32[1]{0:T(128)} %bitcast.section_ref, bf16[768,1792]{1,0:T(8,128)(2,1)S(1)} %bitcast.42, f32[1,7168]{1,0:T(1,128)} %gain_ref.3, bf16[192,192]{1,0:T(8,128)(2,1)} %constant.16.clone.order_ref, bf16[192,192]{1,0:T(8,128)(2,1)} %constant.17.clone.back_ref, bf16[7168,512]{1,0:T(8,128)(2,1)S(1)} %bitcast.23, ...), custom_call_target="tpu_custom_call" | custom-call | flops 8455716864 | bytes 44040192 | tf_op jit(solution)/shard_map/experts/pallas_call | solution.py:366
  69.5 0.0 collective-permute-done.3.other_ref
  69.5 0.0 copy-start.1
  69.6 0.0 copy-start.2
  69.6 6.3 %all-to-all-start.1 = ((bf16[64,24,896]{2,1,0:T(8,128)(2,1)}), bf16[64,24,896]{2,1,0:T(8,128)(2,1)S(1)}, u32[]{:S(2)}, u32[]{:S(2)}) async-start(bf16[64,24,896]{2,1,0:T(8,128)(2,1)} %bitcast.51), calls=%async_computation.1 | async-start | bytes 5505024 | tf_op jit(solution)/shard_map/all_to_all | solution.py:330
  75.9 0.0 copy-start.3
  76.0 0.9 copy-done.3
  76.9 0.8 copy-done.4
  77.7 2.2 %routing.1 = (bf16[2,768,256]{2,1,0:T(8,128)(2,1)S(1)}, bf16[2,512,768]{2,1,0:T(8,128)(2,1)S(1)}, bf16[1,512,768]{2,1,0:T(8,128)(2,1)S(1)}) custom-call(s32[1]{0:T(128)} %bitcast.section_ref, s32[2,2,64]{2,1,0:T(2,128)S(1)} %bitcast.48, f32[2,2,64]{2,1,0:T(2,128)S(1)} %bitcast.50, bf16[16,128]{1,0:T(8,128)(2,1)S(1)} %slice.3.cross_ref, ...), custom_call_target="tpu_custom_call" | custom-call | flops 786432000 | bytes 3145728 | tf_op jit(solution)/shard_map/routing/pallas_call | solution.py:399
  79.9 1.2 copy-done.5
  81.1 0.9 copy-done.6
  82.0 29.5 %all-to-all-done.1 = bf16[64,24,896]{2,1,0:T(8,128)(2,1)S(1)} async-done(((bf16[64,24,896]{2,1,0:T(8,128)(2,1)}), bf16[64,24,896]{2,1,0:T(8,128)(2,1)S(1)}, u32[]{:S(2)}, u32[]{:S(2)}) %all-to-all-start.1) | async-done | bytes 2752544 | tf_op jit(solution)/shard_map/all_to_all | solution.py:330
  111.5 0.0 slice-start.11
  111.5 5.3 %turn.1 = (bf16[1536,896]{1,0:T(8,128)(2,1)S(1)}, bf16[64,3584]{1,0:T(8,128)(2,1)}, bf16[64,3584]{1,0:T(8,128)(2,1)}) custom-call(s32[1]{0:T(128)} %bitcast.section_ref, bf16[64,7168]{1,0:T(8,128)(2,1)} %bitcast.54, bf16[80,3584]{1,0:T(8,128)(2,1)} %copy-done.7, bf16[2,512,768]{2,1,0:T(8,128)(2,1)} %copy-done.5, bf16[1536,896]{1,0:T(8,128)(2,1)S(1)} %bitcast.44, ...), custom_call_target="tpu_custom_call" | custom-call | flops 20000000000 | bytes 7340032 | tf_op jit(solution)/shard_map/turn/pallas_call | solution.py:414
  116.8 41.9 %all_to_all.47 = bf16[64,24,896]{2,1,0:T(8,128)(2,1)S(1)} all-to-all(bf16[64,24,896]{2,1,0:T(8,128)(2,1)S(1)} %bitcast.45), channel_id=1, replica_groups={{0,2,4,6,16,18,20,22,32,34,36,38,48,50,52,54,8,10,12,14,24,26,28,30,40,..., dimensions={0} | all-to-all | bytes 5505024 | tf_op jit(solution)/shard_map/all_to_all | solution.py:330
  158.7 0.7 collective-permute-start.4
  159.4 17.8 %experts.3 = bf16[768,1792]{1,0:T(8,128)(2,1)} custom-call(s32[1]{0:T(128)} %bitcast.section_ref, bf16[1536,896]{1,0:T(8,128)(2,1)S(1)} %bitcast.43, f32[1,7168]{1,0:T(1,128)} %gain_ref.3, bf16[192,192]{1,0:T(8,128)(2,1)} %constant.16.clone.order_ref, bf16[192,192]{1,0:T(8,128)(2,1)} %constant.17.clone.back_ref, bf16[7168,512]{1,0:T(8,128)(2,1)S(1)} %bitcast.26, ...), custom_call_target="tpu_custom_call" | custom-call | flops 8455716864 | bytes 44040192 | tf_op jit(solution)/shard_map/experts/pallas_call | solution.py:366
  177.2 0.0 collective-permute-done.4.first_ref
  177.3 36.7 %all_to_all.48 = bf16[32,24,1792]{2,1,0:T(8,128)(2,1)S(1)} all-to-all(bf16[32,24,1792]{2,1,0:T(8,128)(2,1)} %bitcast.52), channel_id=1, replica_groups={{0,2,4,6,16,18,20,22,32,34,36,38,48,50,52,54,8,10,12,14,24,26,28,30,40,..., dimensions={0} | all-to-all | bytes 5505024 | tf_op jit(solution)/shard_map/all_to_all | solution.py:330
  213.9 2.5 %combine.1 = bf16[64,7168]{1,0:T(8,128)(2,1)} custom-call(bf16[64,3584]{1,0:T(8,128)(2,1)S(1)} %collective-permute-done.4.first_ref, bf16[64,3584]{1,0:T(8,128)(2,1)S(1)} %copy-done, bf16[1,512,768]{2,1,0:T(8,128)(2,1)S(1)} %get-tuple-element.35.weights_ref, bf16[768,1792]{1,0:T(8,128)(2,1)S(1)} %bitcast.41), custom_call_target="tpu_custom_call" | custom-call | flops 1409286144 | bytes 4587520 | tf_op jit(solution)/shard_map/combine/pallas_call | solution.py:434
  (38 shorter events, 0.1 us)
Async XLA Ops:
  0.0 51.3 %collective-permute-start = (bf16[7168,512]{1,0:T(8,128)(2,1)}, bf16[7168,512]{1,0:T(8,128)(2,1)}, u32[]{:S(2)}, u32[]{:S(2)}) collective-permute-start(bf16[7168,512]{1,0:T(8,128)(2,1)} %bitcast.20), channel_id=1, source_target_pairs={{0,1},{1,0},{2,3},{3,2},{4,5},{5,4},{6,7},{7,6},{8,9},{9,8},{10,11... | collective-permute-start | bytes 22020104 | tf_op jit(solution)/shard_map/ppermute | solution.py:333
  0.0 51.3 %collective-permute-start.1 = (bf16[7168,512]{1,0:T(8,128)(2,1)}, bf16[7168,512]{1,0:T(8,128)(2,1)}, u32[]{:S(2)}, u32[]{:S(2)}) collective-permute-start(bf16[7168,512]{1,0:T(8,128)(2,1)} %bitcast.27), channel_id=1, source_target_pairs={{0,1},{1,0},{2,3},{3,2},{4,5},{5,4},{6,7},{7,6},{8,9},{9,8},{10,11... | collective-permute-start | bytes 22020104 | tf_op jit(solution)/shard_map/ppermute | solution.py:333
  0.5 50.8 %collective-permute-start.2 = (bf16[512,7168]{1,0:T(8,128)(2,1)}, bf16[512,7168]{1,0:T(8,128)(2,1)}, u32[]{:S(2)}, u32[]{:S(2)}) collective-permute-start(bf16[512,7168]{1,0:T(8,128)(2,1)} %bitcast.34), channel_id=1, source_target_pairs={{0,1},{1,0},{2,3},{3,2},{4,5},{5,4},{6,7},{7,6},{8,9},{9,8},{10,11... | collective-permute-start | bytes 22020104 | tf_op jit(solution)/shard_map/ppermute | solution.py:333
  0.5 50.8 %slice-start = ((s8[7340032]{0:T(1024)(128)(4,1)}), s8[4194304]{0:T(1024)(128)(4,1)S(1)}, s32[]{:S(2)}) async-start(s8[7340032]{0:T(1024)(128)(4,1)} %bitcast.21), calls=%async_computation.4 | async-start | bytes 8388608
  0.5 50.8 %slice-start.4 = ((s8[7340032]{0:T(1024)(128)(4,1)}), s8[4194304]{0:T(1024)(128)(4,1)S(1)}, s32[]{:S(2)}) async-start(s8[7340032]{0:T(1024)(128)(4,1)} %bitcast.28), calls=%async_computation.8 | async-start | bytes 8388608
  0.5 50.8 %slice-start.8 = ((s8[7340032]{0:T(1024)(128)(4,1)}), s8[4194304]{0:T(1024)(128)(4,1)S(1)}, s32[]{:S(2)}) async-start(s8[7340032]{0:T(1024)(128)(4,1)} %bitcast.35), calls=%async_computation.12 | async-start | bytes 8388608
  0.5 50.8 %slice-start.1 = ((s8[7340032]{0:T(1024)(128)(4,1)}), s8[3145728]{0:T(1024)(128)(4,1)S(1)}, s32[]{:S(2)}) async-start(s8[7340032]{0:T(1024)(128)(4,1)} %bitcast.21), calls=%async_computation.5 | async-start | bytes 6291456
  0.5 50.8 %slice-start.5 = ((s8[7340032]{0:T(1024)(128)(4,1)}), s8[3145728]{0:T(1024)(128)(4,1)S(1)}, s32[]{:S(2)}) async-start(s8[7340032]{0:T(1024)(128)(4,1)} %bitcast.28), calls=%async_computation.9 | async-start | bytes 6291456
  0.5 50.8 %slice-start.9 = ((s8[7340032]{0:T(1024)(128)(4,1)}), s8[3145728]{0:T(1024)(128)(4,1)S(1)}, s32[]{:S(2)}) async-start(s8[7340032]{0:T(1024)(128)(4,1)} %bitcast.35), calls=%async_computation.13 | async-start | bytes 6291456
  48.4 21.1 %collective-permute-start.3 = (bf16[80,3584]{1,0:T(8,128)(2,1)S(1)}, bf16[80,3584]{1,0:T(8,128)(2,1)S(1)}, u32[]{:S(2)}, u32[]{:S(2)}) collective-permute-start(bf16[80,3584]{1,0:T(8,128)(2,1)S(1)} %get-tuple-element.24), channel_id=1, source_target_pairs={{0,64},{64,0},{1,65},{65,1},{2,66},{66,2},{3,67},{67,3},{4,68},{68... | collective-permute-start | bytes 1720328 | tf_op jit(solution)/shard_map/ppermute | solution.py:397
  69.5 6.4 %copy-start.7 = (bf16[80,3584]{1,0:T(8,128)(2,1)}, bf16[80,3584]{1,0:T(8,128)(2,1)S(1)}, u32[]{:S(2)}) copy-start(bf16[80,3584]{1,0:T(8,128)(2,1)S(1)} %collective-permute-done.3.other_ref) | copy-start | bytes 1720324
  69.5 6.4 %copy-start.1 = (s32[1,2,64,2]{2,3,1,0:T(2,128)S(1)}, s32[1,2,64,2]{2,3,1,0:T(2,128)}, u32[]{:S(2)}) copy-start(s32[1,2,64,2]{2,3,1,0:T(2,128)} %param.13) | copy-start | bytes 3076
  69.6 6.4 %copy-start.2 = (f32[1,2,64,2]{2,3,1,0:T(2,128)S(1)}, f32[1,2,64,2]{2,3,1,0:T(2,128)}, u32[]{:S(2)}) copy-start(f32[1,2,64,2]{2,3,1,0:T(2,128)} %param.14) | copy-start | bytes 3076
  69.6 41.9 %all-to-all-start.1 = ((bf16[64,24,896]{2,1,0:T(8,128)(2,1)}), bf16[64,24,896]{2,1,0:T(8,128)(2,1)S(1)}, u32[]{:S(2)}, u32[]{:S(2)}) async-start(bf16[64,24,896]{2,1,0:T(8,128)(2,1)} %bitcast.51), calls=%async_computation.1 | async-start | bytes 5505024 | tf_op jit(solution)/shard_map/all_to_all | solution.py:330
  75.9 0.9 copy-start.3
  76.9 0.8 copy-start.4
  79.9 1.2 copy-start.5
  81.1 0.9 copy-start.6
  111.5 47.8 %slice-start.2 = ((s8[7340032]{0:T(1024)(128)(4,1)}), s8[4194304]{0:T(1024)(128)(4,1)S(1)}, s32[]{:S(2)}) async-start(s8[7340032]{0:T(1024)(128)(4,1)} %bitcast.24), calls=%async_computation.6 | async-start | bytes 8388608
  111.5 47.8 %slice-start.6 = ((s8[7340032]{0:T(1024)(128)(4,1)}), s8[4194304]{0:T(1024)(128)(4,1)S(1)}, s32[]{:S(2)}) async-start(s8[7340032]{0:T(1024)(128)(4,1)} %bitcast.31), calls=%async_computation.10 | async-start | bytes 8388608
  111.5 47.8 %slice-start.10 = ((s8[7340032]{0:T(1024)(128)(4,1)}), s8[4194304]{0:T(1024)(128)(4,1)S(1)}, s32[]{:S(2)}) async-start(s8[7340032]{0:T(1024)(128)(4,1)} %bitcast.38), calls=%async_computation.14 | async-start | bytes 8388608
  111.5 47.8 %slice-start.3 = ((s8[7340032]{0:T(1024)(128)(4,1)}), s8[3145728]{0:T(1024)(128)(4,1)S(1)}, s32[]{:S(2)}) async-start(s8[7340032]{0:T(1024)(128)(4,1)} %bitcast.24), calls=%async_computation.7 | async-start | bytes 6291456
  111.5 47.8 %slice-start.7 = ((s8[7340032]{0:T(1024)(128)(4,1)}), s8[3145728]{0:T(1024)(128)(4,1)S(1)}, s32[]{:S(2)}) async-start(s8[7340032]{0:T(1024)(128)(4,1)} %bitcast.31), calls=%async_computation.11 | async-start | bytes 6291456
  111.5 47.8 %slice-start.11 = ((s8[7340032]{0:T(1024)(128)(4,1)}), s8[3145728]{0:T(1024)(128)(4,1)S(1)}, s32[]{:S(2)}) async-start(s8[7340032]{0:T(1024)(128)(4,1)} %bitcast.38), calls=%async_computation.15 | async-start | bytes 6291456
  116.8 41.9 %copy-start.8 = (bf16[64,3584]{1,0:T(8,128)(2,1)S(1)}, bf16[64,3584]{1,0:T(8,128)(2,1)}, u32[]{:S(2)}) copy-start(bf16[64,3584]{1,0:T(8,128)(2,1)} %get-tuple-element.32) | copy-start | bytes 1376260
  158.7 18.6 %collective-permute-start.4 = (bf16[64,3584]{1,0:T(8,128)(2,1)S(1)}, bf16[64,3584]{1,0:T(8,128)(2,1)S(1)}, u32[]{:S(2)}, u32[]{:S(2)}) collective-permute-start(bf16[64,3584]{1,0:T(8,128)(2,1)S(1)} %copy-done.8), channel_id=1, source_target_pairs={{0,64},{64,0},{1,65},{65,1},{2,66},{66,2},{3,67},{67,3},{4,68},{68... | collective-permute-start | bytes 1376264 | tf_op jit(solution)/shard_map/ppermute | solution.py:431
  177.3 36.7 %copy-start = (bf16[64,3584]{1,0:T(8,128)(2,1)S(1)}, bf16[64,3584]{1,0:T(8,128)(2,1)}, u32[]{:S(2)}) copy-start(bf16[64,3584]{1,0:T(8,128)(2,1)} %get-tuple-element.34.second_ref) | copy-start | bytes 1376260
